TPU v7x, 32 devices: a whole 2x2x4 slice. The times are simulated.
32 devices in a mesh: section: 2 (over core), wide: 4 (over z), narrow: 4 (over y, x).
Axes of the slice: x: 2, y: 2, z: 4, core: 2. Of those that a mesh axis runs over, the one named last changes fastest.
Arguments:
- block_input: bfloat16 [2, 960, 4096], P(None, 'narrow', 'wide'), may hold values from -6 to 6
- output_cotangent: bfloat16 [2, 960, 4096], P(None, 'narrow', 'wide'), may hold values from -6 to 6
- segment_ids: int32 [2, 4096], P(None, 'wide'), may hold values from 0 to 4, as said below
- first_gain: bfloat16 [2, 960], P('section', 'narrow'), may hold values from 0.25 to 1.75
- w_query: bfloat16 [2, 960, 960], P('section', 'wide', 'narrow'), may hold values from -0.25 to 0.25
- w_key: bfloat16 [2, 960, 320], P('section', 'wide', 'narrow'), may hold values from -0.1875 to 0.1875
- w_value: bfloat16 [2, 960, 320], P('section', 'wide', 'narrow'), may hold values from -0.1875 to 0.1875
- w_out: bfloat16 [2, 960, 960], P('section', 'narrow', 'wide'), may hold values from -1.5 to 1.5
- second_gain: bfloat16 [2, 960], P('section', 'narrow'), may hold values from 0.25 to 1.75
- w_gate: bfloat16 [2, 960, 2560], P('section', 'wide', 'narrow'), may hold values from -0.1875 to 0.1875
- w_up: bfloat16 [2, 960, 2560], P('section', 'wide', 'narrow'), may hold values from -0.1875 to 0.1875
- w_down: bfloat16 [2, 2560, 960], P('section', 'narrow', 'wide'), may hold values from -0.125 to 0.125
Outputs:
- section_outputs: bfloat16 [2, 2, 960, 4096], P('section', None, 'narrow', 'wide')
- input_grads: bfloat16 [2, 2, 960, 4096], P('section', None, 'narrow', 'wide')
- grad_first_gain: float32 [2, 960], P('section', 'narrow')
- grad_query: float32 [2, 960, 960], P('section', 'wide', 'narrow')
- grad_key: float32 [2, 960, 320], P('section', 'wide', 'narrow')
- grad_value: float32 [2, 960, 320], P('section', 'wide', 'narrow')
- grad_out: float32 [2, 960, 960], P('section', 'narrow', 'wide')
- grad_second_gain: float32 [2, 960], P('section', 'narrow')
- grad_gate: float32 [2, 960, 2560], P('section', 'wide', 'narrow')
- grad_up: float32 [2, 960, 2560], P('section', 'wide', 'narrow')
- grad_down: float32 [2, 2560, 960], P('section', 'narrow', 'wide')
Inputs may be any that keep to these rules, and one draw needn't show every extreme that they name: `segment_ids`: within each sequence of 1024 tokens the ids start at 0 and never fall; in each sequence one document begins among its first 256 tokens and ends among its last 256 tokens.
All inputs are finite; a program needn't handle non-finite values.
Results may differ from a plain program's by a relative error of at most 0.04.
Values may be sent and summed in bfloat16 or wider, within the bound.
A program may use at most 256 MiB of HBM per device.

v0:
```python
import jax
import jax.numpy as jnp
from jax import lax
from jax.sharding import PartitionSpec as P

D = 960
HEADS = 15
KV_HEADS = 5
HEAD = 64


EPSILON = 1e-05
ROPE_BASE = 100000.0
NEG_FILL = -1e30
id_levels = 5


def passed_along(shard, axis, by):
    length = lax.axis_size(axis)
    pairs = [(i, i + by) for i in range(length) if 0 <= i + by < length]
    return lax.ppermute(shard, axis, pairs)


def collect(local_parts):
    return (
        lax.all_gather(local_parts[0], "wide", axis=0, tiled=True),
        lax.all_gather(local_parts[1], "wide", axis=0, tiled=True),
        lax.all_gather(local_parts[2], "wide", axis=0, tiled=True),
        lax.all_gather(local_parts[3], "wide", axis=0, tiled=True),
        lax.all_gather(local_parts[4], "wide", axis=0, tiled=True),
        lax.all_gather(local_parts[5], "wide", axis=1, tiled=True),
        lax.all_gather(local_parts[6], "wide", axis=1, tiled=True),
    )


def gather_features(values):
    return lax.all_gather(values, "narrow", axis=1, tiled=True)


def to_blocks(values):
    return lax.all_to_all(values, "narrow", split_axis=0, concat_axis=1, tiled=True)


def to_columns(values):
    return lax.all_to_all(values, "narrow", split_axis=1, concat_axis=0, tiled=True)


def row_total(values):
    return lax.psum(values, "narrow")


def column_sum(values):
    return lax.psum_scatter(
        values.astype(jnp.bfloat16), "narrow", scatter_dimension=1, tiled=True
    ).astype(jnp.float32)


def reduce_grads(values):
    return (
        lax.psum_scatter(
            values[0].astype(jnp.bfloat16), "wide", scatter_dimension=0, tiled=True
        ).astype(jnp.float32),
        lax.psum_scatter(
            values[1].astype(jnp.bfloat16), "wide", scatter_dimension=0, tiled=True
        ).astype(jnp.float32),
        lax.psum_scatter(
            values[2].astype(jnp.bfloat16), "wide", scatter_dimension=0, tiled=True
        ).astype(jnp.float32),
        lax.psum_scatter(
            values[3].astype(jnp.bfloat16), "wide", scatter_dimension=0, tiled=True
        ).astype(jnp.float32),
        lax.psum_scatter(
            values[4].astype(jnp.bfloat16), "wide", scatter_dimension=0, tiled=True
        ).astype(jnp.float32),
        lax.psum_scatter(
            values[5].astype(jnp.bfloat16), "wide", scatter_dimension=1, tiled=True
        ).astype(jnp.float32),
        lax.psum_scatter(
            values[6].astype(jnp.bfloat16), "wide", scatter_dimension=1, tiled=True
        ).astype(jnp.float32),
    )


def reduce_gains(values):
    return lax.psum((values[0], values[1]), "wide")


def product(left, right):
    return jnp.dot(left, right, preferred_element_type=jnp.float32)


def product_left(left, right):
    return lax.dot_general(
        left, right, (((0,), (0,)), ((), ())), preferred_element_type=jnp.float32
    )


def product_right(left, right):
    return lax.dot_general(
        left, right, (((1,), (1,)), ((), ())), preferred_element_type=jnp.float32
    )


def inverse_rms(values):
    return lax.rsqrt(row_total(jnp.sum(values * values, axis=1, keepdims=True)) / D + EPSILON)


def norm_back(grad_normed, source, rstd, gain_share):
    scaled = grad_normed * gain_share
    row_dot = row_total(jnp.sum(scaled * source, axis=1, keepdims=True))
    return rstd * scaled - source * rstd**3 * (row_dot / D)


def tables(segment_row):
    length = segment_row.shape[0]
    levels = jnp.arange(id_levels, dtype=jnp.int32)
    onehot = (segment_row[:, None] == levels[None, :]).astype(jnp.float32)
    counts = jnp.sum(onehot, axis=0)
    starts = jnp.cumsum(counts) - counts
    doc_start = jnp.sum(onehot * starts[None, :], axis=1)
    doc_place = jnp.arange(length, dtype=jnp.float32) - doc_start
    half_head = HEAD // 2
    inverse = ROPE_BASE ** (-jnp.arange(half_head, dtype=jnp.float32) / half_head)
    angles = doc_place[:, None] * inverse[None, :]
    return (jnp.cos(angles), jnp.sin(angles))


def rotate(values, cosine, sine_table):
    row_count = values.shape[0]
    head_count = values.shape[1] // HEAD
    half_head = HEAD // 2
    shaped = values.reshape(row_count, head_count, HEAD)
    first_half = shaped[:, :, :half_head]
    second = shaped[:, :, half_head:]
    cos_part = cosine[:, None, :]
    sin_part = sine_table[:, None, :]
    turned = jnp.concatenate(
        [first_half * cos_part - second * sin_part, second * cos_part + first_half * sin_part],
        axis=2,
    )
    return turned.reshape(row_count, head_count * HEAD)


def masked_scores(query_group, key_group, allowed):
    scores = jnp.einsum(
        "qjd,kd->jqk", query_group, key_group, preferred_element_type=jnp.float32
    ) * HEAD ** (-0.5)
    return jnp.where(allowed[None], scores, NEG_FILL)


def attend(queries, keys_rot, value_all, allowed):
    block_rows = queries.shape[0]
    length = keys_rot.shape[0]
    groups = HEADS // KV_HEADS
    query_groups = queries.reshape(block_rows, KV_HEADS, groups, HEAD)
    key_groups = keys_rot.reshape(length, KV_HEADS, HEAD)
    value_groups = value_all.reshape(length, KV_HEADS, HEAD)
    outputs = []
    log_list = []
    for group_index in range(KV_HEADS):
        scores = masked_scores(query_groups[:, group_index], key_groups[:, group_index], allowed)
        row_top = jnp.max(scores, axis=-1, keepdims=True)
        exp_scores = jnp.exp(scores - row_top)
        row_sum = jnp.sum(exp_scores, axis=-1, keepdims=True)
        probs_low = (exp_scores / row_sum).astype(jnp.bfloat16)
        outputs.append(
            jnp.einsum(
                "jqk,kd->qjd",
                probs_low,
                value_groups[:, group_index],
                preferred_element_type=jnp.float32,
            )
        )
        log_list.append(row_top + jnp.log(row_sum))
    mixed = jnp.stack(outputs, axis=1).reshape(block_rows, HEADS * HEAD).astype(jnp.bfloat16)
    return (mixed, jnp.stack(log_list))


def attend_back(queries, keys_rot, value_all, allowed, log_sums, grad_mixed):
    block_rows = queries.shape[0]
    length = keys_rot.shape[0]
    groups = HEADS // KV_HEADS
    score_scale = HEAD ** (-0.5)
    query_groups = queries.reshape(block_rows, KV_HEADS, groups, HEAD)
    grad_groups = grad_mixed.reshape(block_rows, KV_HEADS, groups, HEAD)
    key_groups = keys_rot.reshape(length, KV_HEADS, HEAD)
    value_groups = value_all.reshape(length, KV_HEADS, HEAD)
    query_list = []
    key_list = []
    value_list = []
    for group_index in range(KV_HEADS):
        query_group = query_groups[:, group_index]
        grad_group = grad_groups[:, group_index]
        key_group = key_groups[:, group_index]
        scores = masked_scores(query_group, key_group, allowed)
        probs_full = jnp.exp(scores - log_sums[group_index])
        grad_probs = jnp.einsum(
            "qjd,kd->jqk",
            grad_group,
            value_groups[:, group_index],
            preferred_element_type=jnp.float32,
        )
        row_delta = jnp.sum(grad_probs * probs_full, axis=-1, keepdims=True)
        grad_scores = (probs_full * (grad_probs - row_delta)).astype(jnp.bfloat16)
        query_list.append(
            jnp.einsum("jqk,kd->qjd", grad_scores, key_group, preferred_element_type=jnp.float32)
            * score_scale
        )
        key_list.append(
            jnp.einsum("jqk,qjd->kd", grad_scores, query_group, preferred_element_type=jnp.float32)
            * score_scale
        )
        value_list.append(
            jnp.einsum(
                "jqk,qjd->kd",
                probs_full.astype(jnp.bfloat16),
                grad_group,
                preferred_element_type=jnp.float32,
            )
        )
    grad_queries = jnp.stack(query_list, axis=1).reshape(block_rows, HEADS * HEAD)
    grad_keys = jnp.stack(key_list, axis=1).reshape(length, KV_HEADS * HEAD)
    grad_values = jnp.stack(value_list, axis=1).reshape(length, KV_HEADS * HEAD)
    return (grad_queries, grad_keys, grad_values)


def forward(block_in, weights, gain_pair, segment_row):
    w_query, w_key, w_value, w_gate, w_up, w_out, w_down = weights
    norm_one, norm_two = gain_pair
    column = lax.axis_index("narrow")
    source = block_in.astype(jnp.float32).T
    length = source.shape[0]
    rstd_one = inverse_rms(source)
    normed = gather_features((source * rstd_one * norm_one).astype(jnp.bfloat16))
    query_cols = product(normed, w_query).astype(jnp.bfloat16)
    key_cols = product(normed, w_key).astype(jnp.bfloat16)
    value_cols = product(normed, w_value).astype(jnp.bfloat16)
    query_block = to_blocks(query_cols)
    key_all, value_all = (
        lax.all_gather(key_cols, "narrow", axis=1, tiled=True),
        lax.all_gather(value_cols, "narrow", axis=1, tiled=True),
    )
    block_rows = query_block.shape[0]
    offset = column * block_rows
    cosine, sine_table = tables(segment_row)
    query_cos = lax.dynamic_slice_in_dim(cosine, offset, block_rows, 0)
    query_sin = lax.dynamic_slice_in_dim(sine_table, offset, block_rows, 0)
    queries = rotate(query_block.astype(jnp.float32), query_cos, query_sin).astype(jnp.bfloat16)
    keys_rot = rotate(key_all.astype(jnp.float32), cosine, sine_table).astype(jnp.bfloat16)
    query_ids = lax.dynamic_slice_in_dim(segment_row, offset, block_rows, 0)
    query_pos = offset + jnp.arange(block_rows, dtype=jnp.int32)
    key_pos = jnp.arange(length, dtype=jnp.int32)
    allowed = (query_ids[:, None] == segment_row[None, :]) & (
        key_pos[None, :] <= query_pos[:, None]
    )
    mixed, log_sums = attend(queries, keys_rot, value_all, allowed)
    mixed_cols = to_columns(mixed)
    middle = source + column_sum(product(mixed_cols, w_out))
    rstd_two = inverse_rms(middle)
    normed_two = gather_features((middle * rstd_two * norm_two).astype(jnp.bfloat16))
    gate_values = product(normed_two, w_gate)
    up_values = product(normed_two, w_up)
    hidden = (jax.nn.silu(gate_values) * up_values).astype(jnp.bfloat16)
    result = middle + column_sum(product(hidden, w_down))
    kept_values = (
        source,
        rstd_one,
        normed,
        queries,
        keys_rot,
        value_all,
        allowed,
        log_sums,
        mixed_cols,
        middle,
        rstd_two,
        normed_two,
        gate_values,
        up_values,
        hidden,
        query_cos,
        query_sin,
        cosine,
        sine_table,
    )
    return (result, kept_values)


def backward(kept_values, grad_out, weights, gain_pair):
    (
        source,
        rstd_one,
        normed,
        queries,
        keys_rot,
        value_all,
        allowed,
        log_sums,
        mixed_cols,
        middle,
        rstd_two,
        normed_two,
        gate_values,
        up_values,
        hidden,
        query_cos,
        query_sin,
        cosine,
        sine_table,
    ) = kept_values
    w_query, w_key, w_value, w_gate, w_up, w_out, w_down = weights
    norm_one, norm_two = gain_pair
    grad_full = gather_features(grad_out)
    grad_w_down = product_left(hidden, grad_full)
    grad_hidden = product_right(grad_full, w_down)
    sigmoid_gate = jax.nn.sigmoid(gate_values)
    grad_gate = (
        grad_hidden * up_values * sigmoid_gate * (1.0 + gate_values * (1.0 - sigmoid_gate))
    ).astype(jnp.bfloat16)
    grad_up = (grad_hidden * gate_values * sigmoid_gate).astype(jnp.bfloat16)
    grad_w_gate = product_left(normed_two, grad_gate)
    grad_w_up = product_left(normed_two, grad_up)
    grad_normed_two = column_sum(product_right(grad_gate, w_gate) + product_right(grad_up, w_up))
    grad_norm_two = jnp.sum(grad_normed_two * middle * rstd_two, axis=0)
    grad_middle = grad_out.astype(jnp.float32) + norm_back(
        grad_normed_two, middle, rstd_two, norm_two
    )
    grad_branch = gather_features(grad_middle.astype(jnp.bfloat16))
    grad_w_out = product_left(mixed_cols, grad_branch)
    grad_mixed = to_blocks(product_right(grad_branch, w_out).astype(jnp.bfloat16))
    grad_queries, grad_keys, grad_values = attend_back(
        queries, keys_rot, value_all, allowed, log_sums, grad_mixed
    )
    grad_query_cols = to_columns(rotate(grad_queries, query_cos, -query_sin).astype(jnp.bfloat16))
    key_back = rotate(grad_keys, cosine, -sine_table)
    key_sums, value_sums = (
        lax.psum_scatter(
            key_back.astype(jnp.bfloat16), "narrow", scatter_dimension=1, tiled=True
        ).astype(jnp.float32),
        lax.psum_scatter(
            grad_values.astype(jnp.bfloat16), "narrow", scatter_dimension=1, tiled=True
        ).astype(jnp.float32),
    )
    grad_key_cols = key_sums.astype(jnp.bfloat16)
    grad_value_cols = value_sums.astype(jnp.bfloat16)
    grad_w_query = product_left(normed, grad_query_cols)
    grad_w_key = product_left(normed, grad_key_cols)
    grad_w_value = product_left(normed, grad_value_cols)
    grad_normed = column_sum(
        product_right(grad_query_cols, w_query)
        + product_right(grad_key_cols, w_key)
        + product_right(grad_value_cols, w_value)
    )
    grad_norm_one = jnp.sum(grad_normed * source * rstd_one, axis=0)
    grad_source = grad_middle + norm_back(grad_normed, source, rstd_one, norm_one)
    weight_terms = (
        grad_w_query,
        grad_w_key,
        grad_w_value,
        grad_w_gate,
        grad_w_up,
        grad_w_out,
        grad_w_down,
    )
    return (grad_source, weight_terms, (grad_norm_one, grad_norm_two))


def local(
    block_input,
    output_cotangent,
    segment_ids,
    first_gain,
    w_query,
    w_key,
    w_value,
    w_out,
    second_gain,
    w_gate,
    w_up,
    w_down,
):
    section_count = lax.axis_size("section")
    section_index = lax.axis_index("section")
    batch_count = block_input.shape[0]
    tick_count = batch_count + section_count - 1
    local_parts = (w_query[0], w_key[0], w_value[0], w_gate[0], w_up[0], w_out[0], w_down[0])
    gain_pair = (first_gain[0].astype(jnp.float32), second_gain[0].astype(jnp.float32))
    incoming = jnp.zeros(block_input.shape[1:], jnp.bfloat16)
    kept_list = []
    output_list = []
    for moment in range(tick_count):
        batch_index = jnp.clip(moment - section_index, 0, batch_count - 1)
        fresh_input = block_input[min(moment, batch_count - 1)]
        block_in = jnp.where(section_index == 0, fresh_input, incoming)
        segment_row = lax.dynamic_index_in_dim(segment_ids, batch_index, 0, keepdims=False)
        weights = collect(local_parts)
        result, kept_values = forward(block_in, weights, gain_pair, segment_row)
        sent_output = result.T.astype(jnp.bfloat16)
        kept_list.append(kept_values)
        output_list.append(sent_output)
        if moment + 1 < tick_count:
            incoming = passed_along(sent_output, "section", 1)
    section_outputs = lax.dynamic_slice_in_dim(
        jnp.stack(output_list), section_index, batch_count, 0
    )
    kept_stack = tuple(
        (
            jnp.stack([entry_tuple[position] for entry_tuple in kept_list])
            for position in range(len(kept_list[0]))
        )
    )
    returning = jnp.zeros(block_input.shape[1:], jnp.bfloat16)
    grad_list = []
    weight_totals = None
    gain_totals = None
    for moment in range(tick_count):
        if moment < batch_count:
            fresh_grad = output_cotangent[moment]
        else:
            fresh_grad = jnp.zeros(block_input.shape[1:], jnp.bfloat16)
        grad_out = jnp.where(section_index == section_count - 1, fresh_grad, returning)
        kept_index = jnp.clip(moment - section_count + 1 + 2 * section_index, 0, tick_count - 1)
        kept_values = tuple(
            (
                lax.dynamic_index_in_dim(stacked, kept_index, 0, keepdims=False)
                for stacked in kept_stack
            )
        )
        weights = collect(local_parts)
        grad_source, weight_terms, gain_terms = backward(
            kept_values, grad_out.T, weights, gain_pair
        )
        grad_sent = grad_source.T.astype(jnp.bfloat16)
        grad_list.append(grad_sent)
        weight_part = reduce_grads(weight_terms)
        gain_part = reduce_gains(gain_terms)
        if weight_totals is None:
            weight_totals = weight_part
            gain_totals = gain_part
        else:
            weight_totals = jax.tree.map(jnp.add, weight_totals, weight_part)
            gain_totals = jax.tree.map(jnp.add, gain_totals, gain_part)
        if moment + 1 < tick_count:
            returning = passed_along(grad_sent, "section", -1)
    input_grads = lax.dynamic_slice_in_dim(
        jnp.stack(grad_list), section_count - 1 - section_index, batch_count, 0
    )
    grad_query, grad_key, grad_value, grad_gate, grad_up, grad_out_w, grad_down = weight_totals
    grad_gain_one, grad_gain_two = gain_totals
    return (
        section_outputs[None],
        input_grads[None],
        grad_gain_one[None],
        grad_query[None],
        grad_key[None],
        grad_value[None],
        grad_out_w[None],
        grad_gain_two[None],
        grad_gate[None],
        grad_up[None],
        grad_down[None],
    )


def solution(mesh):
    in_specs = (
        P(None, "narrow", "wide"),
        P(None, "narrow", "wide"),
        P(None, "wide"),
        P("section", "narrow"),
        P("section", "wide", "narrow"),
        P("section", "wide", "narrow"),
        P("section", "wide", "narrow"),
        P("section", "narrow", "wide"),
        P("section", "narrow"),
        P("section", "wide", "narrow"),
        P("section", "wide", "narrow"),
        P("section", "narrow", "wide"),
    )
    out_specs = (
        P("section", None, "narrow", "wide"),
        P("section", None, "narrow", "wide"),
        P("section", "narrow"),
        P("section", "wide", "narrow"),
        P("section", "wide", "narrow"),
        P("section", "wide", "narrow"),
        P("section", "narrow", "wide"),
        P("section", "narrow"),
        P("section", "wide", "narrow"),
        P("section", "wide", "narrow"),
        P("section", "narrow", "wide"),
    )
    return jax.shard_map(local, mesh=mesh, in_specs=in_specs, out_specs=out_specs, check_vma=False)
```

profile of v0, /device:TPU:0, one launch (start us, length us, event | category | flops | bytes accessed | tf_op | source)
XLA Modules:
  0.0 2196.9 jit_solution(4582236268473558571)
XLA Ops:
  26.9 15.9 all-gather
  43.5 15.8 all-gather.1
  63.6 14.6 all-gather.2
  81.7 12.8 all_gather.52
  134.7 16.8 all-gather.3
  155.2 34.7 %reduce-scatter.58.cloned.1.call-done = bf16[1024,240]{0,1:T(8,128)(2,1)} async-done(((bf16[1024,960]{0,1:T(8,128)(2,1)}), bf16[1024,240]{0,1:T(8,128)(2,1)}) %reduce-scatter.58.cloned.1.call-update) | async-done | bytes 491536 | tf_op jit(solution)/shard_map/reduce_scatter | solution.py:53
  203.9 32.7 %all-gather.25.cloned.1.call-done = bf16[1024,960]{0,1:T(8,128)(2,1)} async-done(((bf16[1024,240]{0,1:T(8,128)(2,1)}), bf16[1024,960]{0,1:T(8,128)(2,1)}) %all-gather.25.cloned.1.call-update) | async-done | bytes 1966096 | tf_op jit(solution)/shard_map/all_gather | solution.py:37
  241.9 27.3 %all-gather.49.cloned.1.call-done = bf16[1,960,640]{2,1,0:T(8,128)(2,1)} async-done(((bf16[1,240,640]{2,1,0:T(8,128)(2,1)}), bf16[1,960,640]{2,1,0:T(8,128)(2,1)}) %all-gather.49.cloned.1.call-update) | async-done | bytes 1228816 | tf_op jit(solution)/shard_map/all_gather | solution.py:30
  275.7 25.3 %all-gather.51.cloned.1.call-done = bf16[1,640,960]{1,2,0:T(8,128)(2,1)} async-done(((bf16[1,640,240]{1,2,0:T(8,128)(2,1)}), bf16[1,640,960]{1,2,0:T(8,128)(2,1)}) %all-gather.51.cloned.1.call-update) | async-done | bytes 1228816 | tf_op jit(solution)/shard_map/all_gather | solution.py:32
  305.8 33.4 %reduce-scatter.60.cloned.1.call-done = bf16[1024,240]{0,1:T(8,128)(2,1)} async-done(((bf16[1024,960]{0,1:T(8,128)(2,1)}), bf16[1024,240]{0,1:T(8,128)(2,1)}) %reduce-scatter.60.cloned.1.call-update) | async-done | bytes 491536 | tf_op jit(solution)/shard_map/reduce_scatter | solution.py:53
  356.4 33.3 %all-gather.27.cloned.1.call-done = bf16[1024,960]{0,1:T(8,128)(2,1)} async-done(((bf16[1024,240]{0,1:T(8,128)(2,1)}), bf16[1024,960]{0,1:T(8,128)(2,1)}) %all-gather.27.cloned.1.call-update) | async-done | bytes 1966096 | tf_op jit(solution)/shard_map/all_gather | solution.py:37
  452.9 33.6 %reduce-scatter.62.cloned.1.call-done = bf16[1024,240]{0,1:T(8,128)(2,1)} async-done(((bf16[1024,960]{0,1:T(8,128)(2,1)}), bf16[1024,240]{0,1:T(8,128)(2,1)}) %reduce-scatter.62.cloned.1.call-update) | async-done | bytes 491536 | tf_op jit(solution)/shard_map/reduce_scatter | solution.py:53
  499.0 34.1 %all-gather.29.cloned.1.call-done = bf16[1024,960]{0,1:T(8,128)(2,1)} async-done(((bf16[1024,240]{0,1:T(8,128)(2,1)}), bf16[1024,960]{0,1:T(8,128)(2,1)}) %all-gather.29.cloned.1.call-update) | async-done | bytes 1966096 | tf_op jit(solution)/shard_map/all_gather | solution.py:37
  547.0 34.0 %reduce-scatter.64.cloned.1.call-done = bf16[1024,240]{0,1:T(8,128)(2,1)} async-done(((bf16[1024,960]{0,1:T(8,128)(2,1)}), bf16[1024,240]{0,1:T(8,128)(2,1)}) %reduce-scatter.64.cloned.1.call-update) | async-done | bytes 491536 | tf_op jit(solution)/shard_map/reduce_scatter | solution.py:53
  598.8 32.9 %all-gather.31.cloned.1.call-done = bf16[1024,960]{0,1:T(8,128)(2,1)} async-done(((bf16[1024,240]{0,1:T(8,128)(2,1)}), bf16[1024,960]{0,1:T(8,128)(2,1)}) %all-gather.31.cloned.1.call-update) | async-done | bytes 1966096 | tf_op jit(solution)/shard_map/all_gather | solution.py:37
  693.1 33.6 %reduce-scatter.66.cloned.1.call-done = bf16[1024,240]{0,1:T(8,128)(2,1)} async-done(((bf16[1024,960]{0,1:T(8,128)(2,1)}), bf16[1024,240]{0,1:T(8,128)(2,1)}) %reduce-scatter.66.cloned.1.call-update) | async-done | bytes 491536 | tf_op jit(solution)/shard_map/reduce_scatter | solution.py:53
  740.4 33.1 %all-gather.33.cloned.1.call-done = bf16[1024,960]{0,1:T(8,128)(2,1)} async-done(((bf16[1024,240]{0,1:T(8,128)(2,1)}), bf16[1024,960]{0,1:T(8,128)(2,1)}) %all-gather.33.cloned.1.call-update) | async-done | bytes 1966096 | tf_op jit(solution)/shard_map/all_gather | solution.py:37
  789.7 19.6 all-gather.35.cloned.1.call-done
  827.3 27.6 %reduce-scatter.70.cloned.1.call-done = bf16[1024,240]{0,1:T(8,128)(2,1)} async-done(((bf16[1024,960]{0,1:T(8,128)(2,1)}), bf16[1024,240]{0,1:T(8,128)(2,1)}) %reduce-scatter.70.cloned.1.call-update) | async-done | bytes 491536 | tf_op jit(solution)/shard_map/reduce_scatter | solution.py:53
  873.9 28.2 %all-gather.37.cloned.1.call-done = bf16[1024,960]{0,1:T(8,128)(2,1)} async-done(((bf16[1024,240]{0,1:T(8,128)(2,1)}), bf16[1024,960]{0,1:T(8,128)(2,1)}) %all-gather.37.cloned.1.call-update) | async-done | bytes 1966096 | tf_op jit(solution)/shard_map/all_gather | solution.py:37
  978.6 22.7 %reduce-scatter.74.cloned.1.call-done = bf16[1024,80]{0,1:T(8,128)(2,1)} async-done(((bf16[1024,320]{0,1:T(8,128)(2,1)}), bf16[1024,80]{0,1:T(8,128)(2,1)}) %reduce-scatter.74.cloned.1.call-update) | async-done | bytes 163856 | tf_op jit(solution)/shard_map/reduce_scatter | solution.py:340
  1012.1 28.8 %reduce-scatter.76.cloned.1.call-done = bf16[1024,240]{0,1:T(8,128)(2,1)} async-done(((bf16[1024,960]{0,1:T(8,128)(2,1)}), bf16[1024,240]{0,1:T(8,128)(2,1)}) %reduce-scatter.76.cloned.1.call-update) | async-done | bytes 491536 | tf_op jit(solution)/shard_map/reduce_scatter | solution.py:53
  1059.9 34.3 %all-gather.39.cloned.1.call-done = bf16[1024,960]{0,1:T(8,128)(2,1)} async-done(((bf16[1024,240]{0,1:T(8,128)(2,1)}), bf16[1024,960]{0,1:T(8,128)(2,1)}) %all-gather.39.cloned.1.call-update) | async-done | bytes 1966096 | tf_op jit(solution)/shard_map/all_gather | solution.py:37
  1105.5 34.0 %reduce-scatter.78.cloned.1.call-done = bf16[1024,240]{0,1:T(8,128)(2,1)} async-done(((bf16[1024,960]{0,1:T(8,128)(2,1)}), bf16[1024,240]{0,1:T(8,128)(2,1)}) %reduce-scatter.78.cloned.1.call-update) | async-done | bytes 491536 | tf_op jit(solution)/shard_map/reduce_scatter | solution.py:53
  1152.7 34.3 %all-gather.41.cloned.1.call-done = bf16[1024,960]{0,1:T(8,128)(2,1)} async-done(((bf16[1024,240]{0,1:T(8,128)(2,1)}), bf16[1024,960]{0,1:T(8,128)(2,1)}) %all-gather.41.cloned.1.call-update) | async-done | bytes 1966096 | tf_op jit(solution)/shard_map/all_gather | solution.py:37
  1252.2 25.0 %reduce-scatter.82.cloned.1.call-done = bf16[1024,80]{0,1:T(8,128)(2,1)} async-done(((bf16[1024,320]{0,1:T(8,128)(2,1)}), bf16[1024,80]{0,1:T(8,128)(2,1)}) %reduce-scatter.82.cloned.1.call-update) | async-done | bytes 163856 | tf_op jit(solution)/shard_map/reduce_scatter | solution.py:340
  1283.3 33.3 %reduce-scatter.84.cloned.1.call-done = bf16[1024,240]{0,1:T(8,128)(2,1)} async-done(((bf16[1024,960]{0,1:T(8,128)(2,1)}), bf16[1024,240]{0,1:T(8,128)(2,1)}) %reduce-scatter.84.cloned.1.call-update) | async-done | bytes 491536 | tf_op jit(solution)/shard_map/reduce_scatter | solution.py:53
  1335.4 34.3 %all-gather.43.cloned.1.call-done = bf16[1024,960]{0,1:T(8,128)(2,1)} async-done(((bf16[1024,240]{0,1:T(8,128)(2,1)}), bf16[1024,960]{0,1:T(8,128)(2,1)}) %all-gather.43.cloned.1.call-update) | async-done | bytes 1966096 | tf_op jit(solution)/shard_map/all_gather | solution.py:37
  1381.1 34.0 %reduce-scatter.86.cloned.1.call-done = bf16[1024,240]{0,1:T(8,128)(2,1)} async-done(((bf16[1024,960]{0,1:T(8,128)(2,1)}), bf16[1024,240]{0,1:T(8,128)(2,1)}) %reduce-scatter.86.cloned.1.call-update) | async-done | bytes 491536 | tf_op jit(solution)/shard_map/reduce_scatter | solution.py:53
  1428.3 34.3 %all-gather.45.cloned.1.call-done = bf16[1024,960]{0,1:T(8,128)(2,1)} async-done(((bf16[1024,240]{0,1:T(8,128)(2,1)}), bf16[1024,960]{0,1:T(8,128)(2,1)}) %all-gather.45.cloned.1.call-update) | async-done | bytes 1966096 | tf_op jit(solution)/shard_map/all_gather | solution.py:37
  1677.1 19.2 reduce-scatter.120.cloned.1.call-done
  1697.8 18.6 reduce-scatter.126.cloned.1.call-done
  1718.0 29.1 %reduce-scatter.112.cloned.1.call-done = bf16[640,240]{0,1:T(8,128)(2,1)} async-done(((bf16[640,960]{0,1:T(8,128)(2,1)}), bf16[640,240]{0,1:T(8,128)(2,1)}) %reduce-scatter.112.cloned.1.call-update) | async-done | bytes 307216 | tf_op jit(solution)/shard_map/reduce_scatter | solution.py:78
  1747.1 31.2 %reduce-scatter.114.cloned.1.call-done = bf16[640,240]{0,1:T(8,128)(2,1)} async-done(((bf16[640,960]{0,1:T(8,128)(2,1)}), bf16[640,240]{0,1:T(8,128)(2,1)}) %reduce-scatter.114.cloned.1.call-update) | async-done | bytes 307216 | tf_op jit(solution)/shard_map/reduce_scatter | solution.py:78
  1778.3 31.1 %reduce-scatter.116.cloned.1.call-done = bf16[640,240]{0,1:T(8,128)(2,1)} async-done(((bf16[640,960]{0,1:T(8,128)(2,1)}), bf16[640,240]{0,1:T(8,128)(2,1)}) %reduce-scatter.116.cloned.1.call-update) | async-done | bytes 307216 | tf_op jit(solution)/shard_map/reduce_scatter | solution.py:78
  1811.4 29.3 %reduce-scatter.100.cloned.1.call-done = bf16[240,640]{1,0:T(8,128)(2,1)} async-done(((bf16[960,640]{1,0:T(8,128)(2,1)}), bf16[240,640]{1,0:T(8,128)(2,1)}) %reduce-scatter.100.cloned.1.call-update) | async-done | bytes 307216 | tf_op jit(solution)/shard_map/reduce_scatter | solution.py:69
  1840.7 31.2 %reduce-scatter.102.cloned.1.call-done = bf16[240,640]{1,0:T(8,128)(2,1)} async-done(((bf16[960,640]{1,0:T(8,128)(2,1)}), bf16[240,640]{1,0:T(8,128)(2,1)}) %reduce-scatter.102.cloned.1.call-update) | async-done | bytes 307216 | tf_op jit(solution)/shard_map/reduce_scatter | solution.py:69
  1871.9 31.2 %reduce-scatter.104.cloned.1.call-done = bf16[240,640]{1,0:T(8,128)(2,1)} async-done(((bf16[960,640]{1,0:T(8,128)(2,1)}), bf16[240,640]{1,0:T(8,128)(2,1)}) %reduce-scatter.104.cloned.1.call-update) | async-done | bytes 307216 | tf_op jit(solution)/shard_map/reduce_scatter | solution.py:69
  1905.2 29.2 %reduce-scatter.106.cloned.1.call-done = bf16[240,640]{1,0:T(8,128)(2,1)} async-done(((bf16[960,640]{1,0:T(8,128)(2,1)}), bf16[240,640]{1,0:T(8,128)(2,1)}) %reduce-scatter.106.cloned.1.call-update) | async-done | bytes 307216 | tf_op jit(solution)/shard_map/reduce_scatter | solution.py:72
  1934.3 31.3 %reduce-scatter.108.cloned.1.call-done = bf16[240,640]{1,0:T(8,128)(2,1)} async-done(((bf16[960,640]{1,0:T(8,128)(2,1)}), bf16[240,640]{1,0:T(8,128)(2,1)}) %reduce-scatter.108.cloned.1.call-update) | async-done | bytes 307216 | tf_op jit(solution)/shard_map/reduce_scatter | solution.py:72
  1965.7 31.1 %reduce-scatter.110.cloned.1.call-done = bf16[240,640]{1,0:T(8,128)(2,1)} async-done(((bf16[960,640]{1,0:T(8,128)(2,1)}), bf16[240,640]{1,0:T(8,128)(2,1)}) %reduce-scatter.110.cloned.1.call-update) | async-done | bytes 307216 | tf_op jit(solution)/shard_map/reduce_scatter | solution.py:72
  2000.1 19.2 reduce-scatter.134.cloned.1.call-done
  2022.7 18.5 reduce-scatter.94.cloned.1.call-done
  2041.2 22.0 %reduce-scatter.96.cloned.1.call-done = bf16[240,240]{1,0:T(8,128)(2,1)} async-done(((bf16[960,240]{1,0:T(8,128)(2,1)}), bf16[240,240]{1,0:T(8,128)(2,1)}) %reduce-scatter.96.cloned.1.call-update) | async-done | bytes 115216 | tf_op jit(solution)/shard_map/reduce_scatter | solution.py:60
  2063.2 21.8 reduce-scatter.98.cloned.1.call-done
  2086.8 19.2 reduce-scatter.122.cloned.1.call-done
  2107.5 18.5 reduce-scatter.128.cloned.1.call-done
  2130.5 31.3 %reduce-scatter.92.cloned.1.call-done = bf16[1024,240]{0,1:T(8,128)(2,1)} async-done(((bf16[1024,960]{0,1:T(8,128)(2,1)}), bf16[1024,240]{0,1:T(8,128)(2,1)}) %reduce-scatter.92.cloned.1.call-update) | async-done | bytes 491536 | tf_op jit(solution)/shard_map/reduce_scatter | solution.py:53
  (1122 shorter events, 858.5 us)
Async XLA Ops:
  8.0 71.6 %all-gather.23.cloned.1.call-start = ((), (), s32[]{:S(2)}) async-start(), calls=%async_computation.51 | async-start | bytes 2457600 | tf_op jit(solution)/shard_map/all_gather | solution.py:37
  155.1 81.5 %all-gather.25.cloned.1.call-start = ((), (), s32[]{:S(2)}) async-start(), calls=%async_computation.53 | async-start | bytes 2457600 | tf_op jit(solution)/shard_map/all_gather | solution.py:37
  202.5 66.6 %all-gather.49.cloned.1.call-start = ((), (), s32[]{:S(2)}) async-start(), calls=%async_computation.94 | async-start | bytes 1536000 | tf_op jit(solution)/shard_map/all_gather | solution.py:30
  203.1 97.9 %all-gather.51.cloned.1.call-start = ((), (), s32[]{:S(2)}) async-start(), calls=%async_computation.95 | async-start | bytes 1536000 | tf_op jit(solution)/shard_map/all_gather | solution.py:32
  203.9 135.4 %reduce-scatter.60.cloned.1.call-start = ((), (), s32[]{:S(2)}) async-start(), calls=%async_computation.54 | async-start | bytes 2457600 | tf_op jit(solution)/shard_map/reduce_scatter | solution.py:53
  305.8 83.9 %all-gather.27.cloned.1.call-start = ((), (), s32[]{:S(2)}) async-start(), calls=%async_computation.55 | async-start | bytes 2457600 | tf_op jit(solution)/shard_map/all_gather | solution.py:37
  420.4 66.0 %reduce-scatter.62.cloned.1.call-start = ((), (), s32[]{:S(2)}) async-start(), calls=%async_computation.56 | async-start | bytes 2457600 | tf_op jit(solution)/shard_map/reduce_scatter | solution.py:53
  452.8 80.3 %all-gather.29.cloned.1.call-start = ((), (), s32[]{:S(2)}) async-start(), calls=%async_computation.57 | async-start | bytes 2457600 | tf_op jit(solution)/shard_map/all_gather | solution.py:37
  499.0 82.1 %reduce-scatter.64.cloned.1.call-start = ((), (), s32[]{:S(2)}) async-start(), calls=%async_computation.58 | async-start | bytes 2457600 | tf_op jit(solution)/shard_map/reduce_scatter | solution.py:53
  547.0 84.7 %all-gather.31.cloned.1.call-start = ((), (), s32[]{:S(2)}) async-start(), calls=%async_computation.59 | async-start | bytes 2457600 | tf_op jit(solution)/shard_map/all_gather | solution.py:37
  693.1 80.4 %all-gather.33.cloned.1.call-start = ((), (), s32[]{:S(2)}) async-start(), calls=%async_computation.61 | async-start | bytes 2457600 | tf_op jit(solution)/shard_map/all_gather | solution.py:37
  739.3 69.9 %all-gather.35.cloned.1.call-start = ((), (), s32[]{:S(2)}) async-start(), calls=%async_computation.63 | async-start | bytes 2457600 | tf_op jit(solution)/shard_map/all_gather | solution.py:37
  740.3 114.7 %reduce-scatter.70.cloned.1.call-start = ((), (), s32[]{:S(2)}) async-start(), calls=%async_computation.64 | async-start | bytes 2457600 | tf_op jit(solution)/shard_map/reduce_scatter | solution.py:53
  820.6 81.6 %all-gather.37.cloned.1.call-start = ((), (), s32[]{:S(2)}) async-start(), calls=%async_computation.65 | async-start | bytes 2457600 | tf_op jit(solution)/shard_map/all_gather | solution.py:37
  959.1 81.8 %reduce-scatter.76.cloned.1.call-start = ((), (), s32[]{:S(2)}) async-start(), calls=%async_computation.68 | async-start | bytes 2457600 | tf_op jit(solution)/shard_map/reduce_scatter | solution.py:53
  1006.8 87.3 %all-gather.39.cloned.1.call-start = ((), (), s32[]{:S(2)}) async-start(), calls=%async_computation.69 | async-start | bytes 2457600 | tf_op jit(solution)/shard_map/all_gather | solution.py:37
  1059.8 79.7 %reduce-scatter.78.cloned.1.call-start = ((), (), s32[]{:S(2)}) async-start(), calls=%async_computation.70 | async-start | bytes 2457600 | tf_op jit(solution)/shard_map/reduce_scatter | solution.py:53
  1105.4 81.5 %all-gather.41.cloned.1.call-start = ((), (), s32[]{:S(2)}) async-start(), calls=%async_computation.71 | async-start | bytes 2457600 | tf_op jit(solution)/shard_map/all_gather | solution.py:37
  1152.6 96.0 %reduce-scatter.80.cloned.1.call-start = ((), (), s32[]{:S(2)}) async-start(), calls=%async_computation.72 | async-start | bytes 819200 | tf_op jit(solution)/shard_map/reduce_scatter | solution.py:337
  1233.5 83.1 %reduce-scatter.84.cloned.1.call-start = ((), (), s32[]{:S(2)}) async-start(), calls=%async_computation.74 | async-start | bytes 2457600 | tf_op jit(solution)/shard_map/reduce_scatter | solution.py:53
  1282.6 87.1 %all-gather.43.cloned.1.call-start = ((), (), s32[]{:S(2)}) async-start(), calls=%async_computation.75 | async-start | bytes 2457600 | tf_op jit(solution)/shard_map/all_gather | solution.py:37
  1335.4 79.7 %reduce-scatter.86.cloned.1.call-start = ((), (), s32[]{:S(2)}) async-start(), calls=%async_computation.76 | async-start | bytes 2457600 | tf_op jit(solution)/shard_map/reduce_scatter | solution.py:53
  1381.1 81.5 %all-gather.45.cloned.1.call-start = ((), (), s32[]{:S(2)}) async-start(), calls=%async_computation.77 | async-start | bytes 2457600 | tf_op jit(solution)/shard_map/all_gather | solution.py:37
  1428.3 213.5 %reduce-scatter.88.cloned.1.call-start = ((), (), s32[]{:S(2)}) async-start(), calls=%async_computation.78 | async-start | bytes 819200 | tf_op jit(solution)/shard_map/reduce_scatter | solution.py:337
  1497.8 151.0 %reduce-scatter.90.cloned.1.call-start = ((), (), s32[]{:S(2)}) async-start(), calls=%async_computation.79 | async-start | bytes 819200 | tf_op jit(solution)/shard_map/reduce_scatter | solution.py:340
  1508.3 149.5 %reduce-scatter.68.cloned.1.call-start = ((), (), s32[]{:S(2)}) async-start(), calls=%async_computation.62 | async-start | bytes 2457600 | tf_op jit(solution)/shard_map/reduce_scatter | solution.py:53
  1513.1 148.9 %reduce-scatter.130.cloned.1.call-start = ((), (), s32[]{:S(2)}) async-start(), calls=%async_computation.102 | async-start | bytes 614400
  1536.6 127.0 %reduce-scatter.118.cloned.1.call-start = ((), (), s32[]{:S(2)}) async-start(), calls=%async_computation.96 | async-start | bytes 307200
  1544.4 120.2 %reduce-scatter.124.cloned.1.call-start = ((), (), s32[]{:S(2)}) async-start(), calls=%async_computation.99 | async-start | bytes 307200
  1547.7 127.8 %reduce-scatter.132.cloned.1.call-start = ((), (), s32[]{:S(2)}) async-start(), calls=%async_computation.103 | async-start | bytes 614400
  1553.0 143.3 %reduce-scatter.120.cloned.1.call-start = ((), (), s32[]{:S(2)}) async-start(), calls=%async_computation.97 | async-start | bytes 307200
  1556.3 160.2 %reduce-scatter.126.cloned.1.call-start = ((), (), s32[]{:S(2)}) async-start(), calls=%async_computation.100 | async-start | bytes 307200
  1563.3 183.8 %reduce-scatter.112.cloned.1.call-start = ((), (), s32[]{:S(2)}) async-start(), calls=%async_computation.90 | async-start | bytes 1536000 | tf_op jit(solution)/shard_map/reduce_scatter | solution.py:78
  1568.0 210.3 %reduce-scatter.114.cloned.1.call-start = ((), (), s32[]{:S(2)}) async-start(), calls=%async_computation.91 | async-start | bytes 1536000 | tf_op jit(solution)/shard_map/reduce_scatter | solution.py:78
  1573.0 236.4 %reduce-scatter.116.cloned.1.call-start = ((), (), s32[]{:S(2)}) async-start(), calls=%async_computation.92 | async-start | bytes 1536000 | tf_op jit(solution)/shard_map/reduce_scatter | solution.py:78
  1577.8 262.9 %reduce-scatter.100.cloned.1.call-start = ((), (), s32[]{:S(2)}) async-start(), calls=%async_computation.84 | async-start | bytes 1536000 | tf_op jit(solution)/shard_map/reduce_scatter | solution.py:69
  1587.0 284.9 %reduce-scatter.102.cloned.1.call-start = ((), (), s32[]{:S(2)}) async-start(), calls=%async_computation.85 | async-start | bytes 1536000 | tf_op jit(solution)/shard_map/reduce_scatter | solution.py:69
  1591.8 311.3 %reduce-scatter.104.cloned.1.call-start = ((), (), s32[]{:S(2)}) async-start(), calls=%async_computation.86 | async-start | bytes 1536000 | tf_op jit(solution)/shard_map/reduce_scatter | solution.py:69
  1596.5 337.8 %reduce-scatter.106.cloned.1.call-start = ((), (), s32[]{:S(2)}) async-start(), calls=%async_computation.87 | async-start | bytes 1536000 | tf_op jit(solution)/shard_map/reduce_scatter | solution.py:72
  1601.3 364.4 %reduce-scatter.108.cloned.1.call-start = ((), (), s32[]{:S(2)}) async-start(), calls=%async_computation.88 | async-start | bytes 1536000 | tf_op jit(solution)/shard_map/reduce_scatter | solution.py:72
  1606.0 390.7 %reduce-scatter.110.cloned.1.call-start = ((), (), s32[]{:S(2)}) async-start(), calls=%async_computation.89 | async-start | bytes 1536000 | tf_op jit(solution)/shard_map/reduce_scatter | solution.py:72
  1610.8 408.5 %reduce-scatter.134.cloned.1.call-start = ((), (), s32[]{:S(2)}) async-start(), calls=%async_computation.104 | async-start | bytes 614400
  1616.3 424.9 %reduce-scatter.94.cloned.1.call-start = ((), (), s32[]{:S(2)}) async-start(), calls=%async_computation.81 | async-start | bytes 614400 | tf_op jit(solution)/shard_map/reduce_scatter | solution.py:60
  1619.5 443.7 %reduce-scatter.96.cloned.1.call-start = ((), (), s32[]{:S(2)}) async-start(), calls=%async_computation.82 | async-start | bytes 614400 | tf_op jit(solution)/shard_map/reduce_scatter | solution.py:60
  1622.8 462.2 %reduce-scatter.98.cloned.1.call-start = ((), (), s32[]{:S(2)}) async-start(), calls=%async_computation.83 | async-start | bytes 614400 | tf_op jit(solution)/shard_map/reduce_scatter | solution.py:60
  1641.7 464.3 %reduce-scatter.122.cloned.1.call-start = ((), (), s32[]{:S(2)}) async-start(), calls=%async_computation.98 | async-start | bytes 307200
  1645.0 481.0 %reduce-scatter.128.cloned.1.call-start = ((), (), s32[]{:S(2)}) async-start(), calls=%async_computation.101 | async-start | bytes 307200
  1652.0 509.7 %reduce-scatter.92.cloned.1.call-start = ((), (), s32[]{:S(2)}) async-start(), calls=%async_computation.80 | async-start | bytes 2457600 | tf_op jit(solution)/shard_map/reduce_scatter | solution.py:53
  (295 other events, 8126.6 us)
Sparse Core Ops, SparseCore 0:
  23.4 33.5 all-gather.22
  154.7 35.2 reduce-scatter.57
  305.9 33.2 reduce-scatter.59
  452.9 33.4 reduce-scatter.61
  597.5 34.1 all-gather.30
  693.2 33.5 reduce-scatter.65
  820.7 34.1 reduce-scatter.69
  946.6 26.3 reduce-scatter.71
  976.1 25.2 reduce-scatter.73
  1059.9 34.1 all-gather.38
  1152.8 34.1 all-gather.40
  1223.8 24.8 reduce-scatter.79
  1251.8 25.3 reduce-scatter.81
  1335.5 34.1 all-gather.42
  1428.4 34.1 all-gather.44
  1497.9 24.8 reduce-scatter.87
  1526.4 25.3 reduce-scatter.89
  1554.7 34.1 reduce-scatter.67
  1591.2 21.2 reduce-scatter.129
  1615.3 18.0 reduce-scatter.117
  1635.6 17.8 reduce-scatter.123
  1655.8 19.5 reduce-scatter.131
  1678.3 17.9 reduce-scatter.119
  1698.5 17.8 reduce-scatter.125
  1718.8 28.2 reduce-scatter.111
  1749.4 28.8 reduce-scatter.113
  1780.5 28.8 reduce-scatter.115
  1811.8 28.8 reduce-scatter.99
  1843.0 28.8 reduce-scatter.101
  1874.2 28.8 reduce-scatter.103
  1905.4 28.8 reduce-scatter.105
  1936.8 28.8 reduce-scatter.107
  1967.8 28.8 reduce-scatter.109
  1999.1 20.0 reduce-scatter.133
  2021.6 19.6 reduce-scatter.93
  2043.4 19.7 reduce-scatter.95
  2065.4 19.6 reduce-scatter.97
  2087.9 18.0 reduce-scatter.121
  2108.1 17.8 reduce-scatter.127
  2129.4 32.2 reduce-scatter.91
Sparse Core Ops, SparseCore 1:
  156.6 32.1 all-gather.46
  202.6 34.0 all-gather.24
  238.1 31.0 all-gather.48
  270.8 30.2 all-gather.50
  355.7 34.0 all-gather.26
  499.0 34.0 all-gather.28
  547.1 33.9 reduce-scatter.63
  739.4 34.0 all-gather.32
  775.2 34.0 all-gather.34
  868.1 34.0 all-gather.36
  1006.9 33.9 reduce-scatter.75
  1105.5 33.9 reduce-scatter.77
  1282.7 33.9 reduce-scatter.83
  1381.1 33.9 reduce-scatter.85
where the time goes:
time: 2210 us; the launch traced here: 2200 us
  waiting for transfers between devices  1270 us (57%)
  blocking collectives  325 us (15%)
  matrix products  317 us (14%)
  other arithmetic  136 us (6%)
  local copies, waits for them, and re-layouts  93.9 us (4%)
  starting transfers between devices  29 us (1%)
    reduce_scatter x12, waiting for transfers between devices, column_sum(): lax.psum_scatter(values.astype(jnp.bfloat16), 'narrow', scatter_dimension...  358 us
    all_gather x12, waiting for transfers between devices, gather_features(): return lax.all_gather(values, 'narrow', axis=1, tiled=True)  351 us
    psum x12, blocking collectives, row_total(): return lax.psum(values, 'narrow')  109 us
    unnamed x63, waiting for transfers between devices  107 us
    reduce_scatter x3, waiting for transfers between devices, reduce_grads(): lax.psum_scatter(values[3].astype(jnp.bfloat16), 'wide', scatter_dimensio...  91.7 us
    reduce_scatter x3, waiting for transfers between devices, reduce_grads(): lax.psum_scatter(values[4].astype(jnp.bfloat16), 'wide', scatter_dimensio...  91.6 us
    reduce_scatter x3, waiting for transfers between devices, reduce_grads(): lax.psum_scatter(values[6].astype(jnp.bfloat16), 'wide', scatter_dimensio...  91.4 us
    dot_general x21, matrix products, product_left(): lax.dot_general(left, right, (((0,), (0,)), ((), ())), preferred_element_...  71.6 us
  transfers between devices with their start and end apart: 63, of which 52 were waited for; matrix products, arithmetic and copies ran while one was open for 13% of the time, Pallas kernels for 0%

commit v1 on v0

v1 whole, which is shorter than its diff:
```python
import functools

import jax
import jax.numpy as jnp
from jax import lax
from jax.experimental import pallas as pl
from jax.experimental.pallas import tpu as pltpu
from jax.sharding import PartitionSpec as P

HEAD = 64
EPSILON = 1e-05
ROPE_BASE = 100000.0
NEG_FILL = -1e30
LOW = jnp.bfloat16
FULL = jnp.float32
SCALE = HEAD ** (-0.5)


def dot(left, right, left_dim, right_dim):
    return lax.dot_general(
        left, right, (((left_dim,), (right_dim,)), ((), ())), preferred_element_type=FULL
    )


def attend_kernel(blocks, groups, q_ref, k_ref, v_ref, mask_ref, mixed_ref, log_ref):
    length = q_ref.shape[1]
    for member in range(groups):
        rows = pl.ds(member * HEAD, HEAD)
        query = q_ref[rows, :]
        scores = []
        for j in range(blocks):
            allowed = mask_ref[pl.ds(j * length, length), :] > 0
            scores.append(jnp.where(allowed, dot(k_ref[j, 0], query, 0, 0) * SCALE, NEG_FILL))
        top = scores[0].max(axis=0, keepdims=True)
        for j in range(1, blocks):
            top = jnp.maximum(top, scores[j].max(axis=0, keepdims=True))
        scores = [jnp.exp(s - top) for s in scores]
        total = sum(s.sum(axis=0, keepdims=True) for s in scores)
        inverse = 1.0 / total
        mixed = sum(
            dot(v_ref[j, 0], (scores[j] * inverse).astype(LOW), 1, 0) for j in range(blocks)
        )
        mixed_ref[rows, :] = mixed.astype(LOW)
        log_ref[0, pl.ds(member, 1), :] = top + jnp.log(total)


def attend_back_kernel(
    blocks, groups, q_ref, k_ref, v_ref, mask_ref, log_ref, grad_ref, dq_ref, dk_ref, dv_ref
):
    length = q_ref.shape[1]
    dk = [0.0] * blocks
    dv = [0.0] * blocks
    for member in range(groups):
        rows = pl.ds(member * HEAD, HEAD)
        query = q_ref[rows, :]
        grad = grad_ref[rows, :]
        logs = log_ref[0, pl.ds(member, 1), :]
        probs = []
        grads = []
        delta = 0.0
        for j in range(blocks):
            allowed = mask_ref[pl.ds(j * length, length), :] > 0
            score = jnp.where(allowed, dot(k_ref[j, 0], query, 0, 0) * SCALE, NEG_FILL)
            prob = jnp.exp(score - logs)
            grad_prob = dot(v_ref[j, 0], grad, 0, 0)
            delta = delta + (prob * grad_prob).sum(axis=0, keepdims=True)
            probs.append(prob)
            grads.append(grad_prob)
        dq = 0.0
        for j in range(blocks):
            low_score = (probs[j] * (grads[j] - delta)).astype(LOW)
            dq = dq + dot(k_ref[j, 0], low_score, 1, 0)
            dk[j] = dk[j] + dot(query, low_score, 1, 1)
            dv[j] = dv[j] + dot(grad, probs[j].astype(LOW), 1, 1)
        dq_ref[rows, :] = dq * SCALE
    for j in range(blocks):
        dk_ref[j, 0] = (dk[j] * SCALE).astype(LOW)
        dv_ref[j, 0] = dv[j].astype(LOW)


def attention_specs(blocks, kv_heads, groups, length):
    head_rows = pl.BlockSpec((groups * HEAD, length), lambda g: (g, 0))
    kv = pl.BlockSpec((blocks, 1, HEAD, length), lambda g: (0, g, 0, 0))
    mask = pl.BlockSpec((blocks * length, length), lambda g: (0, 0))
    logs = pl.BlockSpec((1, groups, length), lambda g: (g, 0, 0))
    return head_rows, kv, mask, logs


def attend(queries, keys, values, mask):
    blocks, kv_heads, _, length = keys.shape
    groups = queries.shape[0] // (kv_heads * HEAD)
    head_rows, kv, mask_spec, logs = attention_specs(blocks, kv_heads, groups, length)
    return pl.pallas_call(
        functools.partial(attend_kernel, blocks, groups),
        grid=(kv_heads,),
        in_specs=[head_rows, kv, kv, mask_spec],
        out_specs=[head_rows, logs],
        out_shape=[
            jax.ShapeDtypeStruct(queries.shape, LOW),
            jax.ShapeDtypeStruct((kv_heads, groups, length), FULL),
        ],
        compiler_params=pltpu.CompilerParams(vmem_limit_bytes=32 << 20),
        cost_estimate=pl.CostEstimate(
            flops=16 * queries.size * blocks * length, bytes_accessed=8 << 20, transcendentals=0
        ),
    )(queries, keys, values, mask)


def attend_back(queries, keys, values, mask, logs, grad):
    blocks, kv_heads, _, length = keys.shape
    groups = queries.shape[0] // (kv_heads * HEAD)
    head_rows, kv, mask_spec, log_spec = attention_specs(blocks, kv_heads, groups, length)
    return pl.pallas_call(
        functools.partial(attend_back_kernel, blocks, groups),
        grid=(kv_heads,),
        in_specs=[head_rows, kv, kv, mask_spec, log_spec, head_rows],
        out_specs=[head_rows, kv, kv],
        out_shape=[
            jax.ShapeDtypeStruct(queries.shape, FULL),
            jax.ShapeDtypeStruct(keys.shape, LOW),
            jax.ShapeDtypeStruct(keys.shape, LOW),
        ],
        compiler_params=pltpu.CompilerParams(vmem_limit_bytes=32 << 20),
        cost_estimate=pl.CostEstimate(
            flops=40 * queries.size * blocks * length, bytes_accessed=8 << 20, transcendentals=0
        ),
    )(queries, keys, values, mask, logs, grad)


def rotate(values, cosine, sine):
    length = values.shape[1]
    shaped = values.reshape(-1, 2, HEAD // 2, length)
    a, b = shaped[:, 0], shaped[:, 1]
    return jnp.stack([a * cosine - b * sine, b * cosine + a * sine], axis=1).reshape(values.shape)


def inverse_rms(values):
    return lax.rsqrt(jnp.mean(values * values, axis=0, keepdims=True) + EPSILON)


def norm_back(grad_normed, source, rstd, gain):
    scaled = grad_normed * gain
    row = jnp.mean(scaled * source, axis=0, keepdims=True)
    return rstd * scaled - source * rstd**3 * row


def reduce_scatter(blocks, axis):
    size = lax.axis_size(axis)
    me = lax.axis_index(axis)
    total = lax.dynamic_index_in_dim(blocks, me, 0, keepdims=False).astype(FULL)
    power = size & (size - 1) == 0
    for step in range(1, size):
        if power:
            pairs = [(i, i ^ step) for i in range(size)]
            target = me ^ step
        else:
            pairs = [(i, (i + step) % size) for i in range(size)]
            target = (me + step) % size
        sent = lax.dynamic_index_in_dim(blocks, target, 0, keepdims=False)
        total = total + lax.ppermute(sent, axis, pairs).astype(FULL)
    return total


def local(
    block_input,
    output_cotangent,
    segment_ids,
    first_gain,
    w_query,
    w_key,
    w_value,
    w_out,
    second_gain,
    w_gate,
    w_up,
    w_down,
):
    everywhere = ("section", "narrow", "wide")
    sections = lax.axis_size("section")
    narrow = lax.axis_size("narrow")
    wide = lax.axis_size("wide")
    core = lax.axis_index("section")
    place = lax.axis_index("narrow")
    features = block_input.shape[1]
    width = features * narrow
    sequence = block_input.shape[2]
    length = sequence // narrow
    q_cols, k_cols, hidden_cols = w_query.shape[2], w_key.shape[2], w_gate.shape[2]
    kv_heads = k_cols * narrow // HEAD
    qkv_cols = q_cols + 2 * k_cols
    half = qkv_cols + q_cols + hidden_cols
    gate_at = qkv_cols + q_cols

    packed = jnp.stack(
        [
            jnp.concatenate([w_query[0], w_key[0], w_value[0], w_out[0].T, w_gate[0]], axis=1),
            jnp.concatenate([w_up[0], w_down[0].T], axis=1),
        ]
    )
    halves = lax.all_to_all(packed, "section", 0, 0, tiled=True)
    weights = [
        lax.all_gather(halves[layer], everywhere, axis=0, tiled=True).reshape(
            2, narrow, width, half
        )
        for layer in range(sections)
    ]

    gains = lax.all_gather(
        jnp.stack([first_gain[0], second_gain[0]]), ("section", "narrow"), axis=0
    ).reshape(sections, narrow, 2, features)
    gains = jnp.transpose(gains, (0, 2, 1, 3)).reshape(sections, 2, width, 1).astype(FULL)

    ends = jnp.stack(
        [
            lax.dynamic_index_in_dim(block_input, core, 0, keepdims=False),
            lax.dynamic_index_in_dim(output_cotangent, core, 0, keepdims=False),
        ]
    ).reshape(2, features, narrow, length)
    ends = lax.all_to_all(jnp.transpose(ends, (2, 0, 1, 3)), "narrow", 0, 0, tiled=True)
    start = ends[:, 0].reshape(width, length)
    cotangent = ends[:, 1].reshape(width, length)

    ids = lax.dynamic_index_in_dim(segment_ids, core, 0, keepdims=False)
    offset = place * length
    own_ids = lax.dynamic_slice_in_dim(ids, offset, length, 0)
    positions = jnp.arange(sequence, dtype=jnp.int32)
    own_positions = offset + jnp.arange(length, dtype=jnp.int32)
    mask = (
        (ids[:, None] == own_ids[None, :]) & (positions[:, None] <= own_positions[None, :])
    ).astype(FULL)
    doc_start = jnp.sum((ids[:, None] < own_ids[None, :]).astype(FULL), axis=0)
    half_head = HEAD // 2
    inverse = ROPE_BASE ** (-jnp.arange(half_head, dtype=FULL) / half_head)
    angles = inverse[:, None] * (own_positions.astype(FULL) - doc_start)[None, :]
    cosine, sine = jnp.cos(angles), jnp.sin(angles)

    def q_part(values, n):
        return values[n * q_cols : (n + 1) * q_cols]

    def k_part(values, n):
        return values[n * k_cols : (n + 1) * k_cols]

    kept = []
    results = []
    source = start.astype(FULL)
    for layer in range(sections):
        first, second = weights[layer][0], weights[layer][1]
        gain_one, gain_two = gains[layer, 0], gains[layer, 1]
        rstd_one = inverse_rms(source)
        normed = (source * rstd_one * gain_one).astype(LOW)
        qkv = [dot(first[n, :, :qkv_cols], normed, 0, 0).astype(LOW) for n in range(narrow)]
        query = jnp.concatenate([b[:q_cols] for b in qkv])
        key = jnp.concatenate([b[q_cols : q_cols + k_cols] for b in qkv])
        value = jnp.concatenate([b[q_cols + k_cols :] for b in qkv])
        queries = rotate(query.astype(FULL), cosine, sine).astype(LOW)
        keys = rotate(key.astype(FULL), cosine, sine).astype(LOW)
        both = lax.all_gather(jnp.stack([keys, value]), "narrow", axis=0)
        both = both.reshape(narrow, 2, kv_heads, HEAD, length)
        key_all, value_all = both[:, 0], both[:, 1]
        mixed, logs = attend(queries, key_all, value_all, mask)
        middle = source
        for n in range(narrow):
            middle = middle + dot(first[n, :, qkv_cols:gate_at], q_part(mixed, n), 1, 0)
        rstd_two = inverse_rms(middle)
        normed_two = (middle * rstd_two * gain_two).astype(LOW)
        gates, ups, hiddens = [], [], []
        result = middle
        for n in range(narrow):
            gate = dot(first[n, :, gate_at:], normed_two, 0, 0)
            up = dot(second[n, :, :hidden_cols], normed_two, 0, 0)
            hidden = (jax.nn.silu(gate) * up).astype(LOW)
            result = result + dot(second[n, :, hidden_cols:], hidden, 1, 0)
            gates.append(gate)
            ups.append(up)
            hiddens.append(hidden)
        result = result.astype(LOW)
        kept.append(
            (source, rstd_one, normed, queries, key_all, value_all, mixed, logs, middle)
            + (rstd_two, normed_two, gates, ups, hiddens)
        )
        results.append(result)
        source = result.astype(FULL)

    input_grads = [None] * sections
    gain_grads = [None] * sections
    weight_shards = [None] * sections
    grad = cotangent
    for layer in reversed(range(sections)):
        first, second = weights[layer][0], weights[layer][1]
        gain_one, gain_two = gains[layer, 0], gains[layer, 1]
        (source, rstd_one, normed, queries, key_all, value_all, mixed, logs, middle) = kept[layer][
            :9
        ]
        rstd_two, normed_two, gates, ups, hiddens = kept[layer][9:]
        grad_normed = 0.0
        gate_terms, second_terms = [], []
        for n in range(narrow):
            grad_hidden = dot(second[n, :, hidden_cols:], grad, 0, 0)
            sig = jax.nn.sigmoid(gates[n])
            grad_gate = (grad_hidden * ups[n] * sig * (1.0 + gates[n] * (1.0 - sig))).astype(LOW)
            grad_up = (grad_hidden * gates[n] * sig).astype(LOW)
            grad_normed = grad_normed + dot(first[n, :, gate_at:], grad_gate, 1, 0)
            grad_normed = grad_normed + dot(second[n, :, :hidden_cols], grad_up, 1, 0)
            gate_terms.append(dot(normed_two, grad_gate, 1, 1).astype(LOW))
            second_terms.append(
                jnp.concatenate(
                    [
                        dot(normed_two, grad_up, 1, 1).astype(LOW),
                        dot(grad, hiddens[n], 1, 1).astype(LOW),
                    ],
                    axis=1,
                )
            )
        grad_gain_two = jnp.sum(grad_normed * middle * rstd_two, axis=1)
        grad_middle = grad.astype(FULL) + norm_back(grad_normed, middle, rstd_two, gain_two)
        branch = grad_middle.astype(LOW)
        grad_mixed = jnp.concatenate(
            [dot(first[n, :, qkv_cols:gate_at], branch, 0, 0).astype(LOW) for n in range(narrow)]
        )
        grad_query, grad_key, grad_value = attend_back(
            queries, key_all, value_all, mask, logs, grad_mixed
        )
        sums = lax.all_to_all(
            jnp.stack([grad_key, grad_value], axis=1), "narrow", 0, 0, tiled=True
        )
        sums = jnp.sum(sums.astype(FULL), axis=0).reshape(2, kv_heads * HEAD, length)
        dq = rotate(grad_query, cosine, -sine).astype(LOW)
        dk = rotate(sums[0], cosine, -sine).astype(LOW)
        dv = sums[1].astype(LOW)
        grad_normed = 0.0
        terms = []
        for n in range(narrow):
            block = jnp.concatenate([q_part(dq, n), k_part(dk, n), k_part(dv, n)])
            grad_normed = grad_normed + dot(first[n, :, :qkv_cols], block, 1, 0)
            first_term = jnp.concatenate(
                [
                    dot(normed, block, 1, 1).astype(LOW),
                    dot(branch, q_part(mixed, n), 1, 1).astype(LOW),
                    gate_terms[n],
                ],
                axis=1,
            )
            terms.append(first_term)
        grad_gain_one = jnp.sum(grad_normed * source * rstd_one, axis=1)
        grad = (grad_middle + norm_back(grad_normed, source, rstd_one, gain_one)).astype(LOW)
        input_grads[layer] = grad
        gain_grads[layer] = jnp.stack([grad_gain_one, grad_gain_two])
        stacked = jnp.stack([jnp.stack(terms), jnp.stack(second_terms)])
        shard = reduce_scatter(stacked, "section").astype(LOW)
        shard = reduce_scatter(shard, "narrow").astype(LOW)
        shard = reduce_scatter(shard.reshape(wide, width // wide, half), "wide")
        weight_shards[layer] = shard.astype(LOW)

    owned = lax.all_to_all(jnp.stack(weight_shards), "section", 0, 0, tiled=True).astype(FULL)
    first, second = owned[0], owned[1]

    gain_total = lax.psum(jnp.stack(gain_grads), everywhere)
    gain_total = lax.dynamic_index_in_dim(gain_total, core, 0, keepdims=False)
    gain_total = lax.dynamic_slice_in_dim(gain_total, place * features, features, 1)

    ends = jnp.stack([jnp.stack(results), jnp.stack(input_grads)], axis=1)
    ends = ends.reshape(sections, 2, narrow, features, length)
    ends = jnp.transpose(ends, (0, 2, 1, 3, 4)).reshape(-1, 2, features, length)
    ends = lax.all_to_all(ends, ("section", "narrow"), 0, 0, tiled=True)
    ends = ends.reshape(sections, narrow, 2, features, length)
    ends = jnp.transpose(ends, (2, 0, 3, 1, 4)).reshape(2, sections, features, sequence)

    k_at, v_at = q_cols, q_cols + k_cols
    return (
        ends[0][None],
        ends[1][None],
        gain_total[0][None],
        first[:, :q_cols][None],
        first[:, k_at:v_at][None],
        first[:, v_at:qkv_cols][None],
        first[:, qkv_cols:gate_at].T[None],
        gain_total[1][None],
        first[:, gate_at:][None],
        second[:, :hidden_cols][None],
        second[:, hidden_cols:].T[None],
    )


def solution(mesh):
    by_rows = P("section", "wide", "narrow")
    by_columns = P("section", "narrow", "wide")
    gain = P("section", "narrow")
    ends = P(None, "narrow", "wide")
    in_specs = (
        (ends, ends, P(None, "wide"), gain)
        + (by_rows, by_rows, by_rows, by_columns, gain)
        + (by_rows, by_rows, by_columns)
    )
    carried = P("section", None, "narrow", "wide")
    out_specs = (
        (carried, carried, gain)
        + (by_rows, by_rows, by_rows, by_columns, gain)
        + (by_rows, by_rows, by_columns)
    )
    return jax.shard_map(local, mesh=mesh, in_specs=in_specs, out_specs=out_specs, check_vma=False)
```

time: 2210 us -> 1100 us (0.50)
  waiting for transfers between devices: 1270 us -> 359 us
  matrix products: 317 us -> 141 us
  blocking collectives: 325 us -> 241 us
  local copies, waits for them, and re-layouts: 93.9 us -> 150 us
  Pallas kernels: 0 us -> 50 us
  other arithmetic: 136 us -> 98 us
    reduce_scatter x30 -> x0, waiting for transfers between devices: 743 us -> none  [the longest x12 358 us: column_sum(): lax.psum_scatter(values.astype(jnp.bfloat16), 'narrow', scatter_dimension...]
    dot_general x168 -> x120, matrix products: 317 us -> 141 us  [dot(): lax.dot_general(left, right, (((left_dim,), (right_dim,)), ((), ())), pre...]
    all_gather x15 -> x4, waiting for transfers between devices: 404 us -> 243 us  [the longest x2 211 us: local(): lax.all_gather(halves[layer], everywhere, axis=0, tiled=True)]
    ppermute x4 -> x14, waiting for transfers between devices: 7.8 us -> 115 us  [reduce_scatter(): total = total + lax.ppermute(sent, axis, pairs).astype(FULL)]
    unnamed x63 -> x4, waiting for transfers between devices: 107 us -> 0.75 us
    all_gather x10 -> x1, blocking collectives: 132 us -> 26.2 us  [local(): lax.all_gather(jnp.stack([first_gain[0], second_gain[0]]), ('section', 'n...]
    psum x13 -> x1, blocking collectives: 122 us -> 205 us  [local(): gain_total = lax.psum(jnp.stack(gain_grads), everywhere)]
    all_to_all x7 -> x2, blocking collectives: 71.6 us -> 10.2 us  [the longest x1 5.53 us: local(): lax.all_to_all(jnp.stack(weight_shards), 'section', 0, 0, tiled=True)]
  transfers between devices with their start and end apart: 63 -> 22, of which waited for: 52 -> 8; matrix products, arithmetic and copies ran while one was open for 13% -> 21% of each run, Pallas kernels for 0% -> 0%
where the time goes in v1:
time: 1100 us; the launch traced here: 1090 us
  waiting for transfers between devices  359 us (33%)
  blocking collectives  241 us (22%)
  local copies, waits for them, and re-layouts  150 us (14%)
  matrix products  141 us (13%)
  other arithmetic  98 us (9%)
  Pallas kernels  50 us (5%)
  starting transfers between devices  34.7 us (3%)
  between operations  17 us (2%)
    all_gather x2, waiting for transfers between devices, local(): lax.all_gather(halves[layer], everywhere, axis=0, tiled=True)  211 us
    psum x1, blocking collectives, local(): gain_total = lax.psum(jnp.stack(gain_grads), everywhere)  205 us
    dot_general x120, matrix products, dot(): lax.dot_general(left, right, (((left_dim,), (right_dim,)), ((), ())), pre...  141 us
    ppermute x14, waiting for transfers between devices, reduce_scatter(): total = total + lax.ppermute(sent, axis, pairs).astype(FULL)  115 us
    concatenate x8, local copies, waits for them, and re-layouts, local(): jnp.concatenate([dot(normed, block, 1, 1).astype(LOW), dot(branch, q_part...  37.9 us
    all_gather x2, waiting for transfers between devices, local(): both = lax.all_gather(jnp.stack([keys, value]), 'narrow', axis=0)  31.8 us
    pallas_call x2, Pallas kernels, attend_back(): pl.pallas_call(functools.partial(attend_back_kernel, blocks, groups), gri...  30.3 us
    unnamed x365, local copies, waits for them, and re-layouts  29.3 us
  transfers between devices with their start and end apart: 22, of which 8 were waited for; matrix products, arithmetic and copies ran while one was open for 21% of the time, Pallas kernels for 0%

profile of v1, /device:TPU:0, one launch (start us, length us, event | category | flops | bytes accessed | tf_op | source)
XLA Modules:
  0.0 1091.1 jit_solution(9805244876034096241)
XLA Ops:
  12.5 4.7 all_to_all.30
  21.2 5.2 all-to-all-start
  26.4 26.2 %all-gather.5 = bf16[8,2,240]{2,1,0:T(2,128)(2,1)S(1)} all-gather(bf16[1,2,240]{2,1,0:T(2,128)(2,1)S(1)} %maximum_bitcast_fusion.19), channel_id=3, replica_groups=mesh['section'=2,'wide'=4,'narrow'=4] {'section','narrow'}, dimensions={0}, use_global_device_ids=true | all-gather | bytes 8640 | tf_op jit(solution)/shard_map/all_gather | solution.py:208
  56.3 98.6 %all-gather.11.cloned.1.call-done = bf16[1,7680,1280]{2,1,0:T(8,128)(2,1)} async-done(((bf16[1,240,1280]{2,1,0:T(8,128)(2,1)}), bf16[1,7680,1280]{2,1,0:T(8,128)(2,1)}) %all-gather.11.cloned.1.call-update) | async-done | bytes 19660816 | tf_op jit(solution)/shard_map/all_gather | solution.py:202
  154.9 11.8 %fusion.126 = (bf16[1,3840,1280]{2,1,0:T(8,128)(2,1)}, bf16[1,3840,1280]{2,1,0:T(8,128)(2,1)S(1)}) fusion(bf16[1,7680,1280]{2,1,0:T(8,128)(2,1)} %all-gather.11.cloned.1.call-done), kind=kLoop, calls=%fused_computation.447 | loop fusion | bytes 39321600 | tf_op jit(solution)/shard_map/slice | solution.py:247
  172.3 112.4 %all-gather.15.cloned.1.call-done = bf16[1,7680,1280]{2,1,0:T(8,128)(2,1)} async-done(((bf16[1,240,1280]{2,1,0:T(8,128)(2,1)}), bf16[1,7680,1280]{2,1,0:T(8,128)(2,1)}) %all-gather.15.cloned.1.call-update) | async-done | bytes 19660816 | tf_op jit(solution)/shard_map/all_gather | solution.py:202
  284.7 15.0 %fusion.125 = (bf16[1,3840,1280]{2,1,0:T(8,128)(2,1)}, bf16[1,3840,1280]{2,1,0:T(8,128)(2,1)}) fusion(bf16[1,7680,1280]{2,1,0:T(8,128)(2,1)} %all-gather.15.cloned.1.call-done), kind=kLoop, calls=%fused_computation.446 | loop fusion | bytes 39321600 | tf_op jit(solution)/shard_map/slice | solution.py:247
  299.8 14.4 %all-gather.13.cloned.1.call-done = bf16[8,320,256]{2,1,0:T(8,128)(2,1)} async-done(((bf16[2,320,256]{2,1,0:T(8,128)(2,1)}), bf16[8,320,256]{2,1,0:T(8,128)(2,1)}) %all-gather.13.cloned.1.call-update) | async-done | bytes 1310736 | tf_op jit(solution)/shard_map/all_gather | solution.py:257
  315.8 9.9 shard_map.203
  350.0 2.7 fusion.49
  352.7 2.7 fusion.46
  355.4 2.7 fusion.43
  358.1 3.0 fusion.39
  361.5 17.5 %all-gather.17.cloned.1.call-done = bf16[8,320,256]{2,1,0:T(8,128)(2,1)} async-done(((bf16[2,320,256]{2,1,0:T(8,128)(2,1)}), bf16[8,320,256]{2,1,0:T(8,128)(2,1)}) %all-gather.17.cloned.1.call-update) | async-done | bytes 1310736 | tf_op jit(solution)/shard_map/all_gather | solution.py:257
  380.6 9.7 shard_map.204
  428.7 15.2 %shard_map.205 = (f32[960,256]{1,0:T(8,128)S(1)}, bf16[4,5,64,256]{3,2,1,0:T(8,128)(2,1)S(1)}, bf16[4,5,64,256]{3,2,1,0:T(8,128)(2,1)S(1)}) custom-call(bf16[960,256]{1,0:T(8,128)(2,1)S(1)} %bitcast.568, bf16[4,5,64,256]{3,2,1,0:T(8,128)(2,1)S(1)} %get-tuple-element.144.k_ref, bf16[4,5,64,256]{3,2,1,0:T(8,128)(2,1)S(1)} %get-tuple-element.143.v_ref, ...), custom_call_target="tpu_custom_call" | custom-call | flops 10066329600 | bytes 8388608 | tf_op jit(solution)/shard_map/pallas_call | solution.py:113
  445.3 4.3 all-to-all-start.2
  456.4 4.9 maximum_bitcast_fusion.3
  479.7 2.5 fusion.63
  528.2 15.1 %shard_map.206 = (f32[960,256]{1,0:T(8,128)S(1)}, bf16[4,5,64,256]{3,2,1,0:T(8,128)(2,1)S(1)}, bf16[4,5,64,256]{3,2,1,0:T(8,128)(2,1)S(1)}) custom-call(bf16[960,256]{1,0:T(8,128)(2,1)S(1)} %bitcast.566, bf16[4,5,64,256]{3,2,1,0:T(8,128)(2,1)S(1)} %copy-done.1, bf16[4,5,64,256]{3,2,1,0:T(8,128)(2,1)S(1)} %get-tuple-element.145.v_ref, ...), custom_call_target="tpu_custom_call" | custom-call | flops 10066329600 | bytes 8388608 | tf_op jit(solution)/shard_map/pallas_call | solution.py:113
  545.7 4.7 all-to-all-start.3
  550.4 4.4 concatenate.135
  554.9 4.9 concatenate.134
  559.8 4.5 concatenate.133
  564.3 4.9 concatenate.132
  569.2 6.8 maximum_bitcast_fusion.2
  576.1 6.8 fusion.3
  588.7 4.7 maximum_bitcast_fusion.1
  620.5 4.8 concatenate.127
  625.2 5.0 concatenate.126
  630.2 4.7 concatenate.124
  634.9 4.7 concatenate.125
  639.7 6.8 maximum_bitcast_fusion
  646.6 7.0 fusion.7
  660.0 15.9 %fusion = bf16[4,960,1280]{2,1,0:T(8,128)(2,1)} fusion(bf16[4,960,1280]{2,1,0:T(8,128)(2,1)} %collective-permute-done.7, s32[]{:T(128)S(6)} %select_n.62, bf16[1,4,960,1280]{3,2,1,0:T(8,128)(2,1)} %copy-done.6, bf16[1,4,960,1280]{3,2,1,0:T(8,128)(2,1)} %maximum_bitcast_fusion.3), kind=kLoop, calls=%fused_computation.9 | loop fusion | flops 24576000 | bytes 39321604 | tf_op jit(solution)/shard_map/convert_element_type | solution.py:349
  675.8 6.3 dynamic-slice_bitcast_fusion.2
  685.7 11.7 %fusion.1 = bf16[4,960,1280]{2,1,0:T(8,128)(2,1)} fusion(bf16[4,960,1280]{2,1,0:T(8,128)(2,1)} %collective-permute-done, s32[]{:T(128)S(6)} %select_n.62, bf16[1,4,960,1280]{3,2,1,0:T(8,128)(2,1)S(1)} %bitcast.576, bf16[1,4,960,1280]{3,2,1,0:T(8,128)(2,1)S(1)} %bitcast.574), kind=kLoop, calls=%fused_computation.11 | loop fusion | flops 24576000 | bytes 39321604 | tf_op jit(solution)/shard_map/convert_element_type | solution.py:349
  697.5 6.5 dynamic-slice_bitcast_fusion.5
  707.4 31.3 %collective-permute-done.8 = bf16[960,1280]{1,0:T(8,128)(2,1)} collective-permute-done((bf16[960,1280]{1,0:T(8,128)(2,1)}, bf16[960,1280]{1,0:T(8,128)(2,1)}, u32[]{:S(2)}, u32[]{:S(2)}) %collective-permute-start.8) | collective-permute-done | bytes 2457632 | tf_op jit(solution)/shard_map/ppermute | solution.py:160
  744.5 4.5 all-to-all-start.4
  749.0 204.9 %psum.7 = f32[2,2,960]{2,1,0:T(2,128)S(1)} all-reduce(f32[2,2,960]{2,1,0:T(2,128)S(1)} %pad_maximum_fusion.46), channel_id=1, replica_groups=mesh['section'=2,'wide'=4,'narrow'=4] {'section','narrow','wide'}, use_global_device_ids=true, to_apply=%region_15.16 | all-reduce | flops 3840 | bytes 30720 | tf_op jit(solution)/shard_map/psum | solution.py:357
  954.6 5.1 fusion.12
  964.3 5.1 fusion.15
  975.1 16.2 %collective-permute-done.11 = bf16[240,1280]{1,0:T(8,128)(2,1)S(1)} collective-permute-done((bf16[240,1280]{1,0:T(8,128)(2,1)S(1)}, bf16[240,1280]{1,0:T(8,128)(2,1)S(1)}, u32[]{:S(2)}, u32[]{:S(2)}) %collective-permute-start.11) | collective-permute-done | bytes 614432 | tf_op jit(solution)/shard_map/ppermute | solution.py:160
  991.3 2.8 fusion.127
  999.6 45.6 %collective-permute-done.12 = bf16[240,1280]{1,0:T(8,128)(2,1)} collective-permute-done((bf16[240,1280]{1,0:T(8,128)(2,1)}, bf16[240,1280]{1,0:T(8,128)(2,1)}, u32[]{:S(2)}, u32[]{:S(2)}) %collective-permute-start.12) | collective-permute-done | bytes 614432 | tf_op jit(solution)/shard_map/ppermute | solution.py:160
  1047.0 22.3 %collective-permute-done.5 = bf16[240,1280]{1,0:T(8,128)(2,1)} collective-permute-done((bf16[240,1280]{1,0:T(8,128)(2,1)}, bf16[240,1280]{1,0:T(8,128)(2,1)}, u32[]{:S(2)}, u32[]{:S(2)}) %collective-permute-start.5) | collective-permute-done | bytes 614432 | tf_op jit(solution)/shard_map/ppermute | solution.py:160
  1071.3 5.5 all_to_all.31
  (673 shorter events, 237.4 us)
Async XLA Ops:
  7.2 147.7 %all-gather.11.cloned.1.call-start = ((), (), s32[]{:S(2)}) async-start(), calls=%async_computation.6 | async-start | bytes 20275200 | tf_op jit(solution)/shard_map/all_gather | solution.py:202
  18.4 266.4 %all-gather.15.cloned.1.call-start = ((), (), s32[]{:S(2)}) async-start(), calls=%async_computation.8 | async-start | bytes 20275200 | tf_op jit(solution)/shard_map/all_gather | solution.py:202
  20.1 32.6 %copy-start.130 = (s32[2,1024]{1,0:T(2,128)S(1)}, s32[2,1024]{1,0:T(2,128)}, u32[]{:S(2)}) copy-start(s32[2,1024]{1,0:T(2,128)} %param.14) | copy-start | bytes 24580
  21.2 33.0 %all-to-all-start = ((bf16[4,2,240,256]{3,2,1,0:T(8,128)(2,1)}), bf16[4,2,240,256]{3,2,1,0:T(8,128)(2,1)S(1)}, u32[]{:S(2)}, u32[]{:S(2)}) async-start(bf16[4,2,240,256]{3,2,1,0:T(8,128)(2,1)} %copy.150), calls=%async_computation | async-start | bytes 1966080 | tf_op jit(solution)/shard_map/all_to_all | solution.py:219
  26.3 287.8 %all-gather.13.cloned.1.call-start = ((), (), s32[]{:S(2)}) async-start(), calls=%async_computation.7 | async-start | bytes 1638400 | tf_op jit(solution)/shard_map/all_gather | solution.py:257
  53.6 275.3 %copy-start.103 = (f32[1,1,960,1]{2,1,0,3:T(1,128)}, f32[1,1,960,1]{2,1,0,3:T(1,128)S(1)}, u32[]{:S(2)}) copy-start(f32[1,1,960,1]{2,1,0,3:T(1,128)S(1)} %get-tuple-element.215) | copy-start | bytes 11524
  53.6 292.9 %copy-start.111 = (f32[1,1,960,1]{2,1,0,3:T(1,128)}, f32[1,1,960,1]{2,1,0,3:T(1,128)S(1)}, u32[]{:S(2)}) copy-start(f32[1,1,960,1]{2,1,0,3:T(1,128)S(1)} %get-tuple-element.214) | copy-start | bytes 11524
  54.1 112.6 %copy-start.23 = (bf16[4,2,240,256]{3,2,1,0:T(8,128)(2,1)}, bf16[4,2,240,256]{3,2,1,0:T(8,128)(2,1)S(1)}, u32[]{:S(2)}) copy-start(bf16[4,2,240,256]{3,2,1,0:T(8,128)(2,1)S(1)} %all-to-all-done) | copy-start | bytes 2949124
  55.0 111.7 %copy-start.119 = (f32[256]{0:T(256)}, f32[256]{0:T(256)S(1)}, u32[]{:S(2)}) copy-start(f32[256]{0:T(256)S(1)} %get-tuple-element.221) | copy-start | bytes 3076
  56.3 370.7 %copy-start.21 = (bf16[4,1,240,256]{3,2,1,0:T(8,128)(2,1)}, bf16[4,1,240,256]{3,2,1,0:T(8,128)(2,1)S(1)}, u32[]{:S(2)}) copy-start(bf16[4,1,240,256]{3,2,1,0:T(8,128)(2,1)S(1)} %get-tuple-element.159) | copy-start | bytes 1474564
  171.5 207.5 %all-gather.17.cloned.1.call-start = ((), (), s32[]{:S(2)}) async-start(), calls=%async_computation.9 | async-start | bytes 1638400 | tf_op jit(solution)/shard_map/all_gather | solution.py:257
  314.2 13.0 %slice-start.15 = ((s8[9830400]{0:T(1024)(128)(4,1)}), s8[4194304]{0:T(1024)(128)(4,1)S(1)}, s32[]{:S(2)}) async-start(s8[9830400]{0:T(1024)(128)(4,1)} %bitcast.604), calls=%async_computation.25 | async-start | bytes 8388608
  361.5 28.8 %copy-start.4 = (bf16[15,2,32,256]{3,2,1,0:T(8,128)(2,1)}, bf16[15,2,32,256]{3,2,1,0:T(8,128)(2,1)S(1)}, u32[]{:S(2)}) copy-start(bf16[15,2,32,256]{3,2,1,0:T(8,128)(2,1)S(1)} %pad_maximum_fusion.9) | copy-start | bytes 1474564
  392.9 13.5 %copy-start.15 = (f32[960,256]{1,0:T(8,128)}, f32[960,256]{1,0:T(8,128)S(1)}, u32[]{:S(2)}) copy-start(f32[960,256]{1,0:T(8,128)S(1)} %get-tuple-element.241) | copy-start | bytes 2949124
  393.0 13.5 %copy-start.106 = (f32[256]{0:T(256)}, f32[256]{0:T(256)S(1)}, u32[]{:S(2)}) copy-start(f32[256]{0:T(256)S(1)} %get-tuple-element.227) | copy-start | bytes 3076
  393.0 13.5 %copy-start.115 = (f32[256]{0:T(256)}, f32[256]{0:T(256)S(1)}, u32[]{:S(2)}) copy-start(f32[256]{0:T(256)S(1)} %get-tuple-element.226) | copy-start | bytes 3076
  393.2 27.2 %copy-start.10 = (bf16[960,256]{1,0:T(8,128)(2,1)}, bf16[960,256]{1,0:T(8,128)(2,1)S(1)}, u32[]{:S(2)}) copy-start(bf16[960,256]{1,0:T(8,128)(2,1)S(1)} %multiply_convert_fusion) | copy-start | bytes 1474564
  397.2 29.8 %copy-start.64 = (bf16[640,256]{1,0:T(8,128)(2,1)}, bf16[640,256]{1,0:T(8,128)(2,1)S(1)}, u32[]{:S(2)}) copy-start(bf16[640,256]{1,0:T(8,128)(2,1)S(1)} %get-tuple-element.132) | copy-start | bytes 983044
  399.7 22.3 %copy-start.62 = (bf16[640,256]{1,0:T(8,128)(2,1)}, bf16[640,256]{1,0:T(8,128)(2,1)S(1)}, u32[]{:S(2)}) copy-start(bf16[640,256]{1,0:T(8,128)(2,1)S(1)} %get-tuple-element.123) | copy-start | bytes 983044
  400.9 22.8 %copy-start.66 = (bf16[640,256]{1,0:T(8,128)(2,1)}, bf16[640,256]{1,0:T(8,128)(2,1)S(1)}, u32[]{:S(2)}) copy-start(bf16[640,256]{1,0:T(8,128)(2,1)S(1)} %get-tuple-element.126) | copy-start | bytes 983044
  401.6 23.7 %copy-start.68 = (bf16[640,256]{1,0:T(8,128)(2,1)}, bf16[640,256]{1,0:T(8,128)(2,1)S(1)}, u32[]{:S(2)}) copy-start(bf16[640,256]{1,0:T(8,128)(2,1)S(1)} %get-tuple-element.129) | copy-start | bytes 983044
  445.3 21.7 %all-to-all-start.2 = ((bf16[4,2,5,64,256]{4,3,2,1,0:T(8,128)(2,1)}), bf16[4,2,5,64,256]{4,3,2,1,0:T(8,128)(2,1)}, u32[]{:S(2)}, u32[]{:S(2)}) async-start(bf16[4,2,5,64,256]{4,3,2,1,0:T(8,128)(2,1)} %copy.159), calls=%async_computation.2 | async-start | bytes 2621440 | tf_op jit(solution)/shard_map/all_to_all | solution.py:323
  475.0 14.8 %slice-start.24 = ((s8[9830400]{0:T(1024)(128)(4,1)}), s8[4194304]{0:T(1024)(128)(4,1)S(1)}, s32[]{:S(2)}) async-start(s8[9830400]{0:T(1024)(128)(4,1)} %bitcast.633), calls=%async_computation.34 | async-start | bytes 8388608
  483.2 18.1 %copy-start.19 = (bf16[960,256]{1,0:T(8,128)(2,1)}, bf16[960,256]{1,0:T(8,128)(2,1)S(1)}, u32[]{:S(2)}) copy-start(bf16[960,256]{1,0:T(8,128)(2,1)S(1)} %fusion.60) | copy-start | bytes 1474564
  545.7 52.7 %all-to-all-start.3 = ((bf16[4,2,5,64,256]{4,3,2,1,0:T(8,128)(2,1)}), bf16[4,2,5,64,256]{4,3,2,1,0:T(8,128)(2,1)}, u32[]{:S(2)}, u32[]{:S(2)}) async-start(bf16[4,2,5,64,256]{4,3,2,1,0:T(8,128)(2,1)} %copy.160), calls=%async_computation.3 | async-start | bytes 2621440 | tf_op jit(solution)/shard_map/all_to_all | solution.py:323
  583.4 76.6 %collective-permute-start.7 = (bf16[4,960,1280]{2,1,0:T(8,128)(2,1)}, bf16[4,960,1280]{2,1,0:T(8,128)(2,1)}, u32[]{:S(2)}, u32[]{:S(2)}) collective-permute-start(bf16[4,960,1280]{2,1,0:T(8,128)(2,1)} %fusion.3), channel_id=1, source_target_pairs={{0,16},{16,0},{1,17},{17,1},{2,18},{18,2},{3,19},{19,3},{4,20},{20... | collective-permute-start | bytes 29491208 | tf_op jit(solution)/shard_map/ppermute | solution.py:160
  653.5 32.1 %collective-permute-start = (bf16[4,960,1280]{2,1,0:T(8,128)(2,1)}, bf16[4,960,1280]{2,1,0:T(8,128)(2,1)}, u32[]{:S(2)}, u32[]{:S(2)}) collective-permute-start(bf16[4,960,1280]{2,1,0:T(8,128)(2,1)} %fusion.7), channel_id=1, source_target_pairs={{0,16},{16,0},{1,17},{17,1},{2,18},{18,2},{3,19},{19,3},{4,20},{20... | collective-permute-start | bytes 29491208 | tf_op jit(solution)/shard_map/ppermute | solution.py:160
  657.9 27.8 %slice-start.6 = ((s8[9830400]{0:T(1024)(128)(4,1)}), s8[4194304]{0:T(1024)(128)(4,1)S(1)}, s32[]{:S(2)}) async-start(s8[9830400]{0:T(1024)(128)(4,1)} %bitcast.573), calls=%async_computation.16 | async-start | bytes 8388608
  657.9 27.8 %slice-start.9 = ((s8[9830400]{0:T(1024)(128)(4,1)}), s8[4194304]{0:T(1024)(128)(4,1)S(1)}, s32[]{:S(2)}) async-start(s8[9830400]{0:T(1024)(128)(4,1)} %bitcast.575), calls=%async_computation.19 | async-start | bytes 8388608
  659.9 25.7 %slice-start.7 = ((s8[9830400]{0:T(1024)(128)(4,1)}), s8[4194304]{0:T(1024)(128)(4,1)S(1)}, s32[]{:S(2)}) async-start(s8[9830400]{0:T(1024)(128)(4,1)} %bitcast.573), calls=%async_computation.17 | async-start | bytes 8388608
  659.9 25.7 %slice-start.8 = ((s8[9830400]{0:T(1024)(128)(4,1)}), s8[1441792]{0:T(1024)(128)(4,1)S(1)}, s32[]{:S(2)}) async-start(s8[9830400]{0:T(1024)(128)(4,1)} %bitcast.573), calls=%async_computation.18 | async-start | bytes 2883584
  660.0 25.7 %slice-start.10 = ((s8[9830400]{0:T(1024)(128)(4,1)}), s8[4194304]{0:T(1024)(128)(4,1)S(1)}, s32[]{:S(2)}) async-start(s8[9830400]{0:T(1024)(128)(4,1)} %bitcast.575), calls=%async_computation.20 | async-start | bytes 8388608
  660.0 25.7 %slice-start.11 = ((s8[9830400]{0:T(1024)(128)(4,1)}), s8[1441792]{0:T(1024)(128)(4,1)S(1)}, s32[]{:S(2)}) async-start(s8[9830400]{0:T(1024)(128)(4,1)} %bitcast.575), calls=%async_computation.21 | async-start | bytes 2883584
  682.2 56.5 %collective-permute-start.8 = (bf16[960,1280]{1,0:T(8,128)(2,1)}, bf16[960,1280]{1,0:T(8,128)(2,1)}, u32[]{:S(2)}, u32[]{:S(2)}) collective-permute-start(bf16[960,1280]{1,0:T(8,128)(2,1)} %get-tuple-element.99), channel_id=1, source_target_pairs={{0,1},{1,0},{2,3},{3,2},{4,5},{5,4},{6,7},{7,6},{8,9},{9,8},{10,11... | collective-permute-start | bytes 7372808 | tf_op jit(solution)/shard_map/ppermute | solution.py:160
  684.2 270.4 %collective-permute-start.10 = (bf16[960,1280]{1,0:T(8,128)(2,1)}, bf16[960,1280]{1,0:T(8,128)(2,1)}, u32[]{:S(2)}, u32[]{:S(2)}) collective-permute-start(bf16[960,1280]{1,0:T(8,128)(2,1)} %get-tuple-element.100), channel_id=1, source_target_pairs={{0,3},{1,2},{2,1},{3,0},{4,7},{5,6},{6,5},{7,4},{8,11},{9,10},{10,... | collective-permute-start | bytes 7372808 | tf_op jit(solution)/shard_map/ppermute | solution.py:160
  685.6 268.9 %collective-permute-start.9 = (bf16[960,1280]{1,0:T(8,128)(2,1)}, bf16[960,1280]{1,0:T(8,128)(2,1)}, u32[]{:S(2)}, u32[]{:S(2)}) collective-permute-start(bf16[960,1280]{1,0:T(8,128)(2,1)} %get-tuple-element.101), channel_id=1, source_target_pairs={{0,2},{1,3},{2,0},{3,1},{4,6},{5,7},{6,4},{7,5},{8,10},{9,11},{10,... | collective-permute-start | bytes 7372808 | tf_op jit(solution)/shard_map/ppermute | solution.py:160
  697.4 43.3 %copy-start.63 = (bf16[640,256]{1,0:T(8,128)(2,1)S(1)}, bf16[640,256]{1,0:T(8,128)(2,1)}, u32[]{:S(2)}) copy-start(bf16[640,256]{1,0:T(8,128)(2,1)} %copy-done.62) | copy-start | bytes 983044
  703.9 38.6 %copy-start.53 = (bf16[960,256]{1,0:T(8,128)(2,1)S(1)}, bf16[960,256]{1,0:T(8,128)(2,1)}, u32[]{:S(2)}) copy-start(bf16[960,256]{1,0:T(8,128)(2,1)} %copy-done.50) | copy-start | bytes 1474564
  703.9 258.9 %collective-permute-start.1 = (bf16[960,1280]{1,0:T(8,128)(2,1)}, bf16[960,1280]{1,0:T(8,128)(2,1)}, u32[]{:S(2)}, u32[]{:S(2)}) collective-permute-start(bf16[960,1280]{1,0:T(8,128)(2,1)} %get-tuple-element.96), channel_id=1, source_target_pairs={{0,1},{1,0},{2,3},{3,2},{4,5},{5,4},{6,7},{7,6},{8,9},{9,8},{10,11... | collective-permute-start | bytes 7372808 | tf_op jit(solution)/shard_map/ppermute | solution.py:160
  705.9 258.4 %collective-permute-start.3 = (bf16[960,1280]{1,0:T(8,128)(2,1)}, bf16[960,1280]{1,0:T(8,128)(2,1)}, u32[]{:S(2)}, u32[]{:S(2)}) collective-permute-start(bf16[960,1280]{1,0:T(8,128)(2,1)} %get-tuple-element.97), channel_id=1, source_target_pairs={{0,3},{1,2},{2,1},{3,0},{4,7},{5,6},{6,5},{7,4},{8,11},{9,10},{10,... | collective-permute-start | bytes 7372808 | tf_op jit(solution)/shard_map/ppermute | solution.py:160
  738.7 225.6 %collective-permute-start.2 = (bf16[960,1280]{1,0:T(8,128)(2,1)}, bf16[960,1280]{1,0:T(8,128)(2,1)}, u32[]{:S(2)}, u32[]{:S(2)}) collective-permute-start(bf16[960,1280]{1,0:T(8,128)(2,1)} %get-tuple-element.98), channel_id=1, source_target_pairs={{0,2},{1,3},{2,0},{3,1},{4,6},{5,7},{6,4},{7,5},{8,10},{9,11},{10,... | collective-permute-start | bytes 7372808 | tf_op jit(solution)/shard_map/ppermute | solution.py:160
  744.5 246.7 %all-to-all-start.4 = ((bf16[8,2,240,256]{3,2,1,0:T(8,128)(2,1)}), bf16[8,2,240,256]{3,2,1,0:T(8,128)(2,1)}, u32[]{:S(2)}, u32[]{:S(2)}) async-start(bf16[8,2,240,256]{3,2,1,0:T(8,128)(2,1)} %bitcast.108), calls=%async_computation.4 | async-start | bytes 3932160 | tf_op jit(solution)/shard_map/all_to_all | solution.py:364
  960.8 30.4 %collective-permute-start.11 = (bf16[240,1280]{1,0:T(8,128)(2,1)S(1)}, bf16[240,1280]{1,0:T(8,128)(2,1)S(1)}, u32[]{:S(2)}, u32[]{:S(2)}) collective-permute-start(bf16[240,1280]{1,0:T(8,128)(2,1)S(1)} %get-tuple-element.107), channel_id=1, source_target_pairs={{0,4},{4,0},{8,12},{12,8},{1,5},{5,1},{9,13},{13,9},{2,6},{6,2},{1... | collective-permute-start | bytes 1843208 | tf_op jit(solution)/shard_map/ppermute | solution.py:160
  961.3 38.3 %collective-permute-start.13 = (bf16[240,1280]{1,0:T(8,128)(2,1)}, bf16[240,1280]{1,0:T(8,128)(2,1)}, u32[]{:S(2)}, u32[]{:S(2)}) collective-permute-start(bf16[240,1280]{1,0:T(8,128)(2,1)} %get-tuple-element.108), channel_id=1, source_target_pairs={{0,12},{4,8},{8,4},{12,0},{1,13},{5,9},{9,5},{13,1},{2,14},{6,10},... | collective-permute-start | bytes 1843208 | tf_op jit(solution)/shard_map/ppermute | solution.py:160
  962.8 82.4 %collective-permute-start.12 = (bf16[240,1280]{1,0:T(8,128)(2,1)}, bf16[240,1280]{1,0:T(8,128)(2,1)}, u32[]{:S(2)}, u32[]{:S(2)}) collective-permute-start(bf16[240,1280]{1,0:T(8,128)(2,1)} %get-tuple-element.109), channel_id=1, source_target_pairs={{0,8},{4,12},{8,0},{12,4},{1,9},{5,13},{9,1},{13,5},{2,10},{6,14},... | collective-permute-start | bytes 1843208 | tf_op jit(solution)/shard_map/ppermute | solution.py:160
  972.2 74.8 %collective-permute-start.4 = (bf16[240,1280]{1,0:T(8,128)(2,1)}, bf16[240,1280]{1,0:T(8,128)(2,1)}, u32[]{:S(2)}, u32[]{:S(2)}) collective-permute-start(bf16[240,1280]{1,0:T(8,128)(2,1)} %get-tuple-element.104), channel_id=1, source_target_pairs={{0,4},{4,0},{8,12},{12,8},{1,5},{5,1},{9,13},{13,9},{2,6},{6,2},{1... | collective-permute-start | bytes 1843208 | tf_op jit(solution)/shard_map/ppermute | solution.py:160
  973.5 73.4 %collective-permute-start.6 = (bf16[240,1280]{1,0:T(8,128)(2,1)}, bf16[240,1280]{1,0:T(8,128)(2,1)}, u32[]{:S(2)}, u32[]{:S(2)}) collective-permute-start(bf16[240,1280]{1,0:T(8,128)(2,1)} %get-tuple-element.105), channel_id=1, source_target_pairs={{0,12},{4,8},{8,4},{12,0},{1,13},{5,9},{9,5},{13,1},{2,14},{6,10},... | collective-permute-start | bytes 1843208 | tf_op jit(solution)/shard_map/ppermute | solution.py:160
  991.2 78.0 %collective-permute-start.5 = (bf16[240,1280]{1,0:T(8,128)(2,1)}, bf16[240,1280]{1,0:T(8,128)(2,1)}, u32[]{:S(2)}, u32[]{:S(2)}) collective-permute-start(bf16[240,1280]{1,0:T(8,128)(2,1)} %get-tuple-element.106), channel_id=1, source_target_pairs={{0,8},{4,12},{8,0},{12,4},{1,9},{5,13},{9,1},{13,5},{2,10},{6,14},... | collective-permute-start | bytes 1843208 | tf_op jit(solution)/shard_map/ppermute | solution.py:160
  (157 other events, 616.6 us)
Sparse Core Ops, SparseCore 0:
  18.5 136.3 all-gather.10
  158.3 126.4 all-gather.14
  287.2 26.9 all-gather.12
  350.1 28.7 all-gather.16
